TPU v7x, 32 devices: a whole 2x2x4 slice. The times are simulated.
32 devices in a mesh: expert: 8 (over z, x), mp: 4 (over y, core).
Axes of the slice: x: 2, y: 2, z: 4, core: 2. Of those that a mesh axis runs over, the one named last changes fastest.
Arguments:
- tokens: bfloat16 [2048, 768], P('expert', 'mp'), may hold values from -6 to 6
- gain_one: bfloat16 [768], P('mp'), may hold values from 0.5 to 1.5
- gain_two: bfloat16 [768], P('mp'), may hold values from 0.5 to 1.5
- w_query: bfloat16 [768, 768], P(None, 'mp'), may hold values from -0.21875 to 0.21875
- w_key: bfloat16 [768, 768], P(None, 'mp'), may hold values from -0.21875 to 0.21875
- w_value: bfloat16 [768, 768], P(None, 'mp'), may hold values from -0.21875 to 0.21875
- w_out: bfloat16 [768, 768], P('mp'), may hold values from -1.75 to 1.75
- bias_table: bfloat16 [32, 12], P(None, 'mp'), may hold values from -4 to 4
- w_router: bfloat16 [768, 8], P('mp'), may hold values from -0.15625 to 0.15625
- w_in: bfloat16 [8, 768, 3072], P('expert', None, 'mp'), may hold values from -0.21875 to 0.21875
- w_exp_out: bfloat16 [8, 3072, 768], P('expert', 'mp'), may hold values from -2.5 to 2.5
- cotangent: bfloat16 [2048, 768], P('expert', 'mp'), may hold values from -6 to 6
- routes: int32 [2048], P('expert'), may hold values from 0 to 7, as said below
- slot_index: int32 [2048], P('expert'), may hold values from 0 to 35
- bucket: int32 [511], replicated, may hold values from 0 to 31
Outputs:
- mixed: bfloat16 [2048, 768], P('expert', 'mp')
- grad_tokens: float32 [2048, 768], P('expert', 'mp')
- grad_gain_one: float32 [768], P('mp')
- grad_gain_two: float32 [768], P('mp')
- grad_query: float32 [768, 768], P(None, 'mp')
- grad_key: float32 [768, 768], P(None, 'mp')
- grad_value: float32 [768, 768], P(None, 'mp')
- grad_out: float32 [768, 768], P('mp')
- grad_table: float32 [32, 12], P(None, 'mp')
- grad_router: float32 [768, 8], P('mp')
- grad_in: float32 [8, 768, 3072], P('expert', None, 'mp')
- grad_exp_out: float32 [8, 3072, 768], P('expert', 'mp')
Inputs may be any that keep to these rules, and one draw needn't show every extreme that they name: Within one sequence no two tokens have the same routes and slot_index. Some experts take 36 tokens from every sequence; slots that no token takes stay empty.
All inputs are finite; a program needn't handle non-finite values.
Results may differ from a plain program's by a relative error of at most 0.017.
Values may be sent and summed in bfloat16 or wider, within the bound.
A program may use at most 128 MiB of HBM per device.

v0:
```python
import jax
import jax.numpy as jnp
from jax import lax
from jax.sharding import PartitionSpec as P

HEAD_DIM = 64


EPSILON = 1e-06


def smooth(inputs):
    return jax.nn.gelu(inputs, approximate=True)


def bias_rows(offsets, first_row, count, length):
    row_ids = first_row + jnp.arange(count, dtype=jnp.int32)
    col_ids = jnp.arange(length, dtype=jnp.int32)
    lookup = col_ids[None, :] - row_ids[:, None] + (length - 1)
    return offsets[:, lookup]


def diagonal_sums(values, totals):
    head_count, row_count, col_count = values.shape
    flipped = values[:, ::-1, :]
    padded = jnp.pad(flipped, ((0, 0), (0, 0), (0, row_count)))
    flat = padded.reshape(head_count, row_count * (col_count + row_count))[
        :, : row_count * (col_count + row_count - 1)
    ]
    skewed = flat.reshape(head_count, row_count, col_count + row_count - 1)
    sums = jnp.sum(skewed, axis=1)
    return totals + sums


def row_sums(values):
    return lax.psum(values.astype(jnp.bfloat16), "mp").astype(jnp.float32)


def whole_rows(share_rows):
    return lax.all_gather(share_rows, "mp", axis=1, tiled=True)


def send_rows(share_rows, target, experts, capacity):
    col_share = share_rows.shape[1]
    buffer = jnp.zeros((experts * capacity, col_share), jnp.bfloat16).at[target].set(share_rows)
    buffer = buffer.reshape(experts, capacity, col_share)
    arrived = lax.all_to_all(buffer, "expert", split_axis=0, concat_axis=0, tiled=True)
    arrived = lax.all_gather(arrived, "mp", axis=2, tiled=True)
    return arrived.reshape(experts * capacity, arrived.shape[2])


def return_share(partial_sum, target, experts, capacity):
    shares = lax.psum_scatter(partial_sum, "mp", scatter_dimension=1, tiled=True)
    shares = shares.astype(jnp.bfloat16).reshape(experts, capacity, shares.shape[1])
    homeward = lax.all_to_all(shares, "expert", split_axis=0, concat_axis=0, tiled=True)
    return homeward.reshape(experts * capacity, homeward.shape[2])[target]


def body(
    tokens,
    gain_one,
    gain_two,
    w_query,
    w_key,
    w_value,
    w_out,
    bias_table,
    w_router,
    w_in,
    w_exp_out,
    cotangent,
    routes,
    slot_index,
    bucket,
):
    length, col_share = tokens.shape
    part_id = lax.axis_index("mp")
    experts = w_router.shape[1]
    capacity = max(2, (length * 9 + 8 * experts - 1) // (8 * experts))
    target = routes * capacity + slot_index
    heads_here = w_query.shape[1] // HEAD_DIM
    factor = HEAD_DIM ** (-0.5)
    block_rows = min(512, length)
    num_blocks = length // block_rows
    x_full, gain_a, gain_b, router_full, cot_full = (
        lax.all_gather(tokens, "mp", axis=1, tiled=True),
        lax.all_gather(gain_one, "mp", axis=0, tiled=True),
        lax.all_gather(gain_two, "mp", axis=0, tiled=True),
        lax.all_gather(w_router, "mp", axis=0, tiled=True),
        lax.all_gather(cotangent, "mp", axis=1, tiled=True),
    )
    model_width = x_full.shape[1]
    x_float = x_full.astype(jnp.float32)
    inv_one = lax.rsqrt(jnp.mean(x_float * x_float, axis=1, keepdims=True) + EPSILON)
    normed_one = (x_float * inv_one * gain_a.astype(jnp.float32)).astype(jnp.bfloat16)
    queries = jnp.dot(normed_one, w_query, preferred_element_type=jnp.float32).astype(jnp.bfloat16)
    keys_all = jnp.dot(normed_one, w_key, preferred_element_type=jnp.float32).astype(jnp.bfloat16)
    values_all = jnp.dot(normed_one, w_value, preferred_element_type=jnp.float32).astype(
        jnp.bfloat16
    )
    key_heads = keys_all.reshape(length, heads_here, HEAD_DIM)
    value_heads = values_all.reshape(length, heads_here, HEAD_DIM)
    query_blocks = queries.reshape(num_blocks, block_rows, heads_here, HEAD_DIM)
    starts = jnp.arange(num_blocks, dtype=jnp.int32) * block_rows
    onehot = (bucket[:, None] == jnp.arange(bias_table.shape[0], dtype=jnp.int32)[None, :]).astype(
        jnp.float32
    )
    offset_bias = jnp.dot(onehot, bias_table.astype(jnp.float32), precision=lax.Precision.HIGHEST).T

    def block_scores(q_block, first_row):
        scores = (
            jnp.einsum("qhd,khd->hqk", q_block, key_heads, preferred_element_type=jnp.float32)
            * factor
        )
        return scores + bias_rows(offset_bias, first_row, block_rows, length)

    def forward_block(pieces):
        q_block, first_row = pieces
        scores = block_scores(q_block, first_row)
        row_peak = jnp.max(scores, axis=2, keepdims=True)
        raised = jnp.exp(scores - row_peak)
        row_total = jnp.sum(raised, axis=2, keepdims=True)
        prob_low = (raised / row_total).astype(jnp.bfloat16)
        blended = jnp.einsum(
            "hqk,khd->qhd", prob_low, value_heads, preferred_element_type=jnp.float32
        )
        return (
            blended.astype(jnp.bfloat16).reshape(block_rows, -1),
            (row_peak + jnp.log(row_total))[:, :, 0],
        )

    attended, log_norm = lax.map(forward_block, (query_blocks, starts))
    attended = attended.reshape(length, -1)
    attn_partial = jnp.dot(attended, w_out, preferred_element_type=jnp.float32)
    picked = (routes[:, None] == jnp.arange(experts, dtype=jnp.int32)[None, :]).astype(jnp.float32)
    resid_one = x_float + lax.psum(attn_partial, "mp")
    inv_two = lax.rsqrt(jnp.mean(resid_one * resid_one, axis=1, keepdims=True) + EPSILON)
    normed_two = (resid_one * inv_two * gain_b.astype(jnp.float32)).astype(jnp.bfloat16)
    logits = jnp.dot(normed_two, router_full, preferred_element_type=jnp.float32)
    normed_share = lax.dynamic_slice_in_dim(normed_two, part_id * col_share, col_share, 1)
    resid_own = lax.dynamic_slice_in_dim(resid_one, part_id * col_share, col_share, 1)
    router_probs = jax.nn.softmax(logits, axis=1)
    gate = jnp.sum(router_probs * picked, axis=1)
    expert_in = send_rows(normed_share, target, experts, capacity)
    pre_act = jnp.dot(expert_in, w_in[0], preferred_element_type=jnp.float32)
    hidden_f, gelu_pull = jax.vjp(smooth, pre_act)
    hidden = hidden_f.astype(jnp.bfloat16)
    returned_share = return_share(
        jnp.dot(hidden, w_exp_out[0], preferred_element_type=jnp.float32), target, experts, capacity
    )
    returned_own = returned_share.astype(jnp.float32)
    mixed_out = (resid_own + gate[:, None] * returned_own).astype(jnp.bfloat16)
    cot_own = cotangent.astype(jnp.float32)
    returned_f = whole_rows(returned_share).astype(jnp.float32)
    cot_float = cot_full.astype(jnp.float32)
    d_gate = jnp.sum(cot_float * returned_f, axis=1)
    d_returned = (gate[:, None] * cot_own).astype(jnp.bfloat16)
    d_expert_out = send_rows(d_returned, target, experts, capacity)
    grad_exp_out = jnp.einsum("rf,rd->fd", hidden, d_expert_out, preferred_element_type=jnp.float32)
    d_hidden = jnp.einsum(
        "rd,fd->rf", d_expert_out, w_exp_out[0], preferred_element_type=jnp.float32
    )
    d_pre = gelu_pull(d_hidden)[0].astype(jnp.bfloat16)
    grad_in = jnp.einsum("rd,rf->df", expert_in, d_pre, preferred_element_type=jnp.float32)
    d_share = return_share(
        jnp.einsum("rf,df->rd", d_pre, w_in[0], preferred_element_type=jnp.float32),
        target,
        experts,
        capacity,
    )
    d_logits = ((d_gate * gate)[:, None] * (picked - router_probs)).astype(jnp.bfloat16)
    d_from_experts = whole_rows(d_share)
    router_grad_full = jnp.einsum(
        "ld,le->de", normed_two, d_logits, preferred_element_type=jnp.float32
    )
    d_normed_two = d_from_experts.astype(jnp.float32) + jnp.einsum(
        "le,de->ld", d_logits, router_full, preferred_element_type=jnp.float32
    )
    hat_two = resid_one * inv_two
    u_two = d_normed_two * gain_b.astype(jnp.float32)
    d_resid = cot_float + inv_two * (
        u_two - hat_two * jnp.mean(u_two * hat_two, axis=1, keepdims=True)
    )
    gain_two_grad = jnp.sum(d_normed_two * hat_two, axis=0)
    d_attn = d_resid.astype(jnp.bfloat16)
    d_resid_own = lax.dynamic_slice_in_dim(d_resid, part_id * col_share, col_share, 1)
    router_own = lax.dynamic_slice_in_dim(router_grad_full, part_id * col_share, col_share, 0)
    gain_two_own = lax.dynamic_slice_in_dim(gain_two_grad, part_id * col_share, col_share, 0)
    grad_out = jnp.einsum("lk,ld->kd", attended, d_attn, preferred_element_type=jnp.float32)
    d_attended = jnp.einsum("ld,kd->lk", d_attn, w_out, preferred_element_type=jnp.float32).astype(
        jnp.bfloat16
    )
    d_blocks = d_attended.reshape(num_blocks, block_rows, heads_here, HEAD_DIM)

    def backward_block(carry, pieces):
        d_keys, d_values, d_offsets = carry
        q_block, d_block, norm_block, first_row = pieces
        scores = block_scores(q_block, first_row)
        probs_full = jnp.exp(scores - norm_block[:, :, None])
        d_probs = jnp.einsum(
            "qhd,khd->hqk", d_block, value_heads, preferred_element_type=jnp.float32
        )
        inner_sum = jnp.sum(d_probs * probs_full, axis=2, keepdims=True)
        d_scores = (probs_full * (d_probs - inner_sum)).astype(jnp.bfloat16)
        d_query = (
            jnp.einsum("hqk,khd->qhd", d_scores, key_heads, preferred_element_type=jnp.float32)
            * factor
        ).astype(jnp.bfloat16)
        d_keys = (
            d_keys
            + jnp.einsum("hqk,qhd->khd", d_scores, q_block, preferred_element_type=jnp.float32)
            * factor
        )
        d_values = d_values + jnp.einsum(
            "hqk,qhd->khd",
            probs_full.astype(jnp.bfloat16),
            d_block,
            preferred_element_type=jnp.float32,
        )
        d_offsets = diagonal_sums(d_scores.astype(jnp.float32), d_offsets)
        return ((d_keys, d_values, d_offsets), d_query.reshape(block_rows, -1))

    zero_heads = jnp.zeros((length, heads_here, HEAD_DIM), jnp.float32)
    carried, d_queries = lax.scan(
        backward_block,
        (zero_heads, zero_heads, jnp.zeros_like(offset_bias)),
        (query_blocks, d_blocks, log_norm, starts),
    )
    d_keys_all = carried[0].reshape(length, -1).astype(jnp.bfloat16)
    d_values_all = carried[1].reshape(length, -1).astype(jnp.bfloat16)
    d_queries = d_queries.reshape(length, -1)
    table_grad = jnp.einsum("ob,ho->bh", onehot, carried[2], precision=lax.Precision.HIGHEST)
    grad_query = jnp.einsum("ld,lk->dk", normed_one, d_queries, preferred_element_type=jnp.float32)
    grad_key = jnp.einsum("ld,lk->dk", normed_one, d_keys_all, preferred_element_type=jnp.float32)
    grad_value = jnp.einsum(
        "ld,lk->dk", normed_one, d_values_all, preferred_element_type=jnp.float32
    )
    d_normed_one = jnp.einsum("lk,dk->ld", d_queries, w_query, preferred_element_type=jnp.float32)
    d_normed_one = d_normed_one + jnp.einsum(
        "lk,dk->ld", d_keys_all, w_key, preferred_element_type=jnp.float32
    )
    d_normed_one = d_normed_one + jnp.einsum(
        "lk,dk->ld", d_values_all, w_value, preferred_element_type=jnp.float32
    )
    d_own = lax.psum_scatter(
        d_normed_one.astype(jnp.bfloat16), "mp", scatter_dimension=1, tiled=True
    ).astype(jnp.float32)
    hat_one = tokens.astype(jnp.float32) * inv_one
    u_one = d_own * gain_one.astype(jnp.float32)
    one_stat = row_sums(jnp.sum(u_one * hat_one, axis=1))
    grad_tokens = d_resid_own + inv_one * (u_one - hat_one * (one_stat[:, None] / model_width))
    gain_one_grad = jnp.sum(d_own * hat_one, axis=0)
    summed = lax.psum(
        (
            grad_query,
            grad_key,
            grad_value,
            grad_out,
            table_grad,
            router_own,
            gain_one_grad,
            gain_two_own,
        ),
        "expert",
    )
    return (
        mixed_out,
        grad_tokens,
        summed[6],
        summed[7],
        summed[0],
        summed[1],
        summed[2],
        summed[3],
        summed[4],
        summed[5],
        grad_in[None],
        grad_exp_out[None],
    )


def solution(mesh):
    return jax.shard_map(
        body,
        mesh=mesh,
        in_specs=(
            P("expert", "mp"),
            P("mp"),
            P("mp"),
            P(None, "mp"),
            P(None, "mp"),
            P(None, "mp"),
            P("mp", None),
            P(None, "mp"),
            P("mp", None),
            P("expert", None, "mp"),
            P("expert", "mp", None),
            P("expert", "mp"),
            P("expert"),
            P("expert"),
            P(),
        ),
        out_specs=(
            P("expert", "mp"),
            P("expert", "mp"),
            P("mp"),
            P("mp"),
            P(None, "mp"),
            P(None, "mp"),
            P(None, "mp"),
            P("mp", None),
            P(None, "mp"),
            P("mp", None),
            P("expert", None, "mp"),
            P("expert", "mp", None),
        ),
        check_vma=False,
    )
```

profile of v0, /device:TPU:0, one launch (start us, length us, event | category | flops | bytes accessed | tf_op | source)
XLA Modules:
  0.0 593.0 jit_solution(15330091218361412095)
XLA Ops:
  7.3 8.3 %all_gather.27 = bf16[256,768]{0,1:T(8,128)(2,1)S(1)} all-gather(bf16[256,192]{0,1:T(8,128)(2,1)} %param.15), channel_id=1, replica_groups=mesh['expert'=8,'mp'=4] {'mp'}, dimensions={1}, use_global_device_ids=true | all-gather | bytes 491520 | tf_op jit(solution)/shard_map/all_gather | solution.py:86
  17.5 6.8 %all-reduce.5 = (bf16[768]{0:T(1024)(128)(2,1)S(1)}, bf16[768]{0:T(1024)(128)(2,1)S(1)}) all-reduce(bf16[768]{0:T(1024)(128)(2,1)S(1)} %dynamic-update-slice, bf16[768]{0:T(1024)(128)(2,1)S(1)} %dynamic-update-slice.1), channel_id=1, replica_groups=mesh['expert'=8,'mp'=4] {'mp'}, use_global_device_ids=true, to_apply=%add.1 | all-reduce | flops 1536 | bytes 6144
  25.1 217.1 %gather_fusion = f32[65536,3]{1,0:T(8,128)} fusion(f32[3,511]{0,1:T(8,128)S(1)} %copy.60, s32[65536]{0:T(1024)S(1)} %broadcast_clamp_fusion), kind=kCustom, calls=%fused_computation | custom fusion | bytes 1835008 | tf_op jit(solution)/shard_map/while/body/eval_jaxpr/gather | solution.py:20
  242.2 19.0 %copy.62 = f32[256,256,3]{0,1,2:T(8,128)S(1)} copy(f32[256,256,3]{2,1,0:T(8,128)} %bitcast.99) | data formatting | bytes 1572864 | tf_op jit(solution)/shard_map/while/body/eval_jaxpr/gather | solution.py:20
  264.2 1.2 fusion.61
  266.1 34.7 %all-reduce.9.cloned.1.call-done = f32[256,768]{1,0:T(8,128)} async-done(((f32[256,768]{1,0:T(8,128)}), f32[256,768]{1,0:T(8,128)}) %all-reduce.9.cloned.1.call-update) | async-done | bytes 786448 | tf_op jit(solution)/shard_map/psum | solution.py:136
  300.8 1.3 multiply_reduce_fusion.3
  302.2 2.3 scatter_custom_fusion
  304.5 1.6 reshape.169
  306.2 13.2 %all_to_all.20 = bf16[8,36,192]{2,1,0:T(8,128)(2,1)} all-to-all(bf16[8,36,192]{2,1,0:T(8,128)(2,1)} %reshape.169), channel_id=1, replica_groups=mesh['expert'=8,'mp'=4] {'expert'}, dimensions={0} | all-to-all | bytes 221184 | tf_op jit(solution)/shard_map/all_to_all | solution.py:47
  319.3 1.9 copy.65
  321.3 14.0 %all_gather.31 = bf16[8,36,768]{1,0,2:T(8,128)(2,1)} all-gather(bf16[8,36,192]{1,0,2:T(8,128)(2,1)} %copy.65), channel_id=1, replica_groups=mesh['expert'=8,'mp'=4] {'mp'}, dimensions={2}, use_global_device_ids=true | all-gather | bytes 552960 | tf_op jit(solution)/shard_map/all_gather | solution.py:48
  335.2 3.2 reshape.239
  338.4 2.0 fusion.7
  341.4 1.9 convolution_bitcast_fusion.3
  343.9 5.2 all-gather.2
  349.7 1.4 reshape.234
  351.1 1.7 copy.68
  355.0 1.9 scatter_custom_fusion.1
  357.0 11.3 %all_to_all.21 = bf16[8,36,192]{2,1,0:T(8,128)(2,1)} all-to-all(bf16[8,36,192]{2,1,0:T(8,128)(2,1)S(1)} %reshape.173), channel_id=1, replica_groups=mesh['expert'=8,'mp'=4] {'expert'}, dimensions={0} | all-to-all | bytes 221184 | tf_op jit(solution)/shard_map/all_to_all | solution.py:47
  368.3 1.2 copy.69
  369.5 13.0 %all_gather.33 = bf16[8,36,768]{1,0,2:T(8,128)(2,1)} all-gather(bf16[8,36,192]{1,0,2:T(8,128)(2,1)S(1)} %copy.69), channel_id=1, replica_groups=mesh['expert'=8,'mp'=4] {'mp'}, dimensions={2}, use_global_device_ids=true | all-gather | bytes 552960 | tf_op jit(solution)/shard_map/all_gather | solution.py:48
  382.5 3.2 reshape.240
  385.7 2.4 fusion.17
  388.8 1.8 convolution_bitcast_fusion.2
  391.5 6.7 %all_gather.32 = bf16[256,768]{0,1:T(8,128)(2,1)S(1)} all-gather(bf16[256,192]{0,1:T(8,128)(2,1)S(1)} %copy-done.24), channel_id=1, replica_groups=mesh['expert'=8,'mp'=4] {'mp'}, dimensions={1}, use_global_device_ids=true | all-gather | bytes 491520 | tf_op jit(solution)/shard_map/all_gather | solution.py:90
  398.5 1.1 copy.92
  400.2 3.4 all-to-all-start.1
  403.7 10.8 %reduce-scatter.12.cloned.1.call-done = f32[192,288]{1,0:T(8,128)} async-done(((f32[768,288]{1,0:T(8,128)}), f32[192,288]{1,0:T(8,128)}) %reduce-scatter.12.cloned.1.call-update) | async-done | bytes 221200
  416.2 5.5 all-to-all-start.3
  421.8 1.2 gather_fusion.1
  423.1 6.1 %all-gather.1 = bf16[256,768]{0,1:T(8,128)(2,1)S(1)} all-gather(bf16[256,192]{0,1:T(8,128)(2,1)S(1)} %copy.73), channel_id=3, replica_groups=mesh['expert'=8,'mp'=4] {'mp'}, dimensions={1}, use_global_device_ids=true | all-gather | bytes 491520 | tf_op jit(solution)/shard_map/all_gather | solution.py:40
  429.7 1.2 gather_fusion.2
  431.0 6.6 %all-gather = bf16[256,768]{0,1:T(8,128)(2,1)S(1)} all-gather(bf16[256,192]{0,1:T(8,128)(2,1)S(1)} %copy.71), channel_id=2, replica_groups=mesh['expert'=8,'mp'=4] {'mp'}, dimensions={1}, use_global_device_ids=true | all-gather | bytes 491520 | tf_op jit(solution)/shard_map/all_gather | solution.py:40
  444.2 1.1 fusion.2
  445.6 1.2 fusion.50
  446.7 1.2 fusion.52
  447.9 1.2 fusion.54
  451.4 2.2 convolution_bitcast_fusion.1
  453.6 2.3 convolution_bitcast_fusion
  459.1 1.1 copy.99
  460.6 2.8 reshape.179
  463.4 1.6 reduce_sum.122
  465.6 1.5 reduce-scatter.14.cloned.1.call-done
  468.3 5.8 psum.71
  475.1 39.1 %all-reduce.3 = (f32[192]{0:T(256)}, f32[192]{0:T(256)}, f32[32,3]{0,1:T(4,128)}, f32[192,8]{0,1:T(8,128)}) all-reduce(f32[192]{0:T(256)S(1)} %get-tuple-element.104, f32[192]{0:T(256)S(1)} %dynamic_slice.33, f32[32,3]{0,1:T(4,128)S(1)} %fusion.35, ...), channel_id=1, replica_groups=mesh['expert'=8,'mp'=4] {'expert'}, use_global_device_ids=true, to_apply=%region_19.20 | all-reduce | flops 2016 | bytes 16128 | tf_op jit(solution)/shard_map/psum | solution.py:253
  514.1 67.9 %all-reduce.11.cloned.1.call-done = (f32[768,192]{0,1:T(8,128)}, f32[768,192]{0,1:T(8,128)}, f32[768,192]{0,1:T(8,128)}, f32[192,768]{1,0:T(8,128)}) async-done(((f32[768,192]{0,1:T(8,128)}, f32[768,192]{0,1:T(8,128)}, f32[768,192]{0,1:T(8,128)}, f32[192,768]{1,0:T(8,128)}), (f32[768,192]{0,1:T(8,128)}, f32[768,192]{0,1:T(8,128)}, f32[768,192]{0,1:T(8,128)}, ...) | async-done | bytes 2359312 | tf_op jit(solution)/shard_map/psum | solution.py:253
  582.0 2.0 copy.109
  (218 shorter events, 33.1 us)
Async XLA Ops:
  7.2 334.2 %copy-start = (bf16[1,768,768]{2,1,0:T(8,128)(2,1)S(1)}, bf16[1,768,768]{2,1,0:T(8,128)(2,1)}, u32[]{:S(2)}) copy-start(bf16[1,768,768]{2,1,0:T(8,128)(2,1)} %param.25) | copy-start | bytes 3538948
  7.2 8.6 %copy-start.64 = (u32[32]{0:T(128)S(1)}, u32[32]{0:T(128)}, u32[]{:S(2)}) copy-start(u32[32]{0:T(128)} %constant.105) | copy-start | bytes 388
  7.2 9.9 %copy-start.62 = (bf16[192]{0:T(256)(128)(2,1)S(1)}, bf16[192]{0:T(256)(128)(2,1)}, u32[]{:S(2)}) copy-start(bf16[192]{0:T(256)(128)(2,1)} %param.16) | copy-start | bytes 1156
  7.2 10.1 %copy-start.61 = (bf16[192]{0:T(256)(128)(2,1)S(1)}, bf16[192]{0:T(256)(128)(2,1)}, u32[]{:S(2)}) copy-start(bf16[192]{0:T(256)(128)(2,1)} %param.17) | copy-start | bytes 1156
  7.2 17.3 %copy-start.60 = (bf16[32,3]{0,1:T(4,128)(2,1)S(1)}, bf16[32,3]{0,1:T(4,128)(2,1)}, u32[]{:S(2)}) copy-start(bf16[32,3]{0,1:T(4,128)(2,1)} %param.22) | copy-start | bytes 580
  7.2 17.3 %copy-start.58 = (s32[511]{0:T(512)S(1)}, s32[511]{0:T(512)}, u32[]{:S(2)}) copy-start(s32[511]{0:T(512)} %param.29) | copy-start | bytes 6136
  7.3 293.5 %all-reduce.9.cloned.1.call-start = ((), (), s32[]{:S(2)}) async-start(), calls=%async_computation.7 | async-start | bytes 1572864 | tf_op jit(solution)/shard_map/psum | solution.py:136
  24.5 237.5 %copy-start.35 = (f32[256]{0:T(256)}, f32[256]{0:T(256)S(1)}, u32[]{:S(2)}) copy-start(f32[256]{0:T(256)S(1)} %add_rsqrt_fusion.1) | copy-start | bytes 3076
  242.2 19.0 %copy-start.30 = (bf16[768,192]{0,1:T(8,128)(2,1)S(1)}, bf16[768,192]{0,1:T(8,128)(2,1)}, u32[]{:S(2)}) copy-start(bf16[768,192]{0,1:T(8,128)(2,1)} %param.20) | copy-start | bytes 884740
  242.2 19.4 %copy-start.26 = (bf16[768,192]{0,1:T(8,128)(2,1)S(1)}, bf16[768,192]{0,1:T(8,128)(2,1)}, u32[]{:S(2)}) copy-start(bf16[768,192]{0,1:T(8,128)(2,1)} %param.18) | copy-start | bytes 884740
  261.6 1.6 copy-start.33
  263.8 2.2 copy-start.18
  263.8 1.6 copy-start.43
  263.8 1.7 copy-start.57
  265.4 133.0 %reduce-scatter.10.cloned.1.call-start = ((), (), s32[]{:S(2)}) async-start(), calls=%async_computation.8 | async-start | bytes 1474560
  302.1 19.2 %copy-start.51 = (f32[256]{0:T(256)}, f32[256]{0:T(256)S(1)}, u32[]{:S(2)}) copy-start(f32[256]{0:T(256)S(1)} %add_rsqrt_fusion) | copy-start | bytes 3076
  302.2 50.5 %copy-start.2 = (bf16[256,768]{1,0:T(8,128)(2,1)}, bf16[256,768]{1,0:T(8,128)(2,1)S(1)}, u32[]{:S(2)}) copy-start(bf16[256,768]{1,0:T(8,128)(2,1)S(1)} %multiply_convert_fusion.2) | copy-start | bytes 1179652
  343.3 71.2 %reduce-scatter.12.cloned.1.call-start = ((), (), s32[]{:S(2)}) async-start(), calls=%async_computation.9 | async-start | bytes 1474560
  355.0 2.0 copy-start.48
  385.7 3.1 copy-start.8
  390.6 7.8 %copy-start.56 = (s32[256]{0:T(256)S(1)}, s32[256]{0:T(256)}, u32[]{:S(2)}) copy-start(s32[256]{0:T(256)} %compare_select_fusion.1) | copy-start | bytes 3076
  391.5 12.1 %copy-start.38 = (f32[3,256]{1,0:T(4,128)S(1)}, f32[3,256]{1,0:T(4,128)}, u32[]{:S(2)}) copy-start(f32[3,256]{1,0:T(4,128)} %copy-done.37) | copy-start | bytes 9220
  391.5 12.1 %copy-start.42 = (f32[3,256]{1,0:T(4,128)S(1)}, f32[3,256]{1,0:T(4,128)}, u32[]{:S(2)}) copy-start(f32[3,256]{1,0:T(4,128)} %copy-done.41) | copy-start | bytes 9220
  400.2 16.0 %all-to-all-start.1 = ((bf16[8,36,192]{2,1,0:T(8,128)(2,1)}), bf16[8,36,192]{2,1,0:T(8,128)(2,1)S(1)}, u32[]{:S(2)}, u32[]{:S(2)}) async-start(bf16[8,36,192]{2,1,0:T(8,128)(2,1)} %reshape.171), calls=%async_computation.1 | async-start | bytes 327680 | tf_op jit(solution)/shard_map/all_to_all | solution.py:55
  416.2 13.4 %all-to-all-start.3 = ((bf16[8,36,192]{2,1,0:T(8,128)(2,1)}), bf16[8,36,192]{2,1,0:T(8,128)(2,1)S(1)}, u32[]{:S(2)}, u32[]{:S(2)}) async-start(bf16[8,36,192]{2,1,0:T(8,128)(2,1)} %reshape.175), calls=%async_computation.3 | async-start | bytes 327680 | tf_op jit(solution)/shard_map/all_to_all | solution.py:55
  421.7 45.4 %reduce-scatter.14.cloned.1.call-start = ((), (), s32[]{:S(2)}) async-start(), calls=%async_computation.10 | async-start | bytes 491520
  423.0 6.6 %copy-start.49 = (f32[256]{0:T(256)S(1)}, f32[256]{0:T(256)}, u32[]{:S(2)}) copy-start(f32[256]{0:T(256)} %copy-done.48) | copy-start | bytes 3076
  429.6 8.1 %copy-start.53 = (f32[256]{0:T(256)}, f32[256]{0:T(256)S(1)}, u32[]{:S(2)}) copy-start(f32[256]{0:T(256)S(1)} %mul.254) | copy-start | bytes 3076
  429.7 8.1 %copy-start.32 = (bf16[768,8]{0,1:T(8,128)(2,1)S(1)}, bf16[768,8]{0,1:T(8,128)(2,1)}, u32[]{:S(2)}) copy-start(bf16[768,8]{0,1:T(8,128)(2,1)} %reshape.234) | copy-start | bytes 36868
  429.7 8.1 %copy-start.40 = (f32[256]{0:T(256)S(1)}, f32[256]{0:T(256)}, u32[]{:S(2)}) copy-start(f32[256]{0:T(256)} %copy-done.39) | copy-start | bytes 3076
  429.7 8.1 %copy-start.44 = (s32[256]{0:T(256)S(1)}, s32[256]{0:T(256)}, u32[]{:S(2)}) copy-start(s32[256]{0:T(256)} %param.27) | copy-start | bytes 3076
  429.7 8.1 %copy-start.46 = (f32[256]{0:T(256)S(1)}, f32[256]{0:T(256)}, u32[]{:S(2)}) copy-start(f32[256]{0:T(256)} %copy-done.45) | copy-start | bytes 3076
  429.7 8.1 %copy-start.52 = (f32[256]{0:T(256)S(1)}, f32[256]{0:T(256)}, u32[]{:S(2)}) copy-start(f32[256]{0:T(256)} %copy-done.51) | copy-start | bytes 3076
  442.4 1.4 copy-start.13
  443.8 1.8 copy-start.36
  444.2 2.5 copy-start.14
  445.3 136.7 %all-reduce.11.cloned.1.call-start = ((), (), s32[]{:S(2)}) async-start(), calls=%async_computation.11 | async-start | bytes 4718592 | tf_op jit(solution)/shard_map/psum | solution.py:253
  446.7 2.3 copy-start.19
  451.4 2.2 copy-start.5
  451.4 2.2 copy-start.12
  463.4 1.6 copy-start.3
  463.4 1.6 copy-start.47
  463.4 1.6 copy-start.54
  463.4 1.9 copy-start.59
  582.0 2.0 copy-start.17
  582.0 2.8 copy-start.16
  584.0 1.6 copy-start.15
  584.1 2.5 copy-start.1
  (24 other events, 21.1 us)
Sparse Core Ops, SparseCore 0:
  265.5 35.1 all-reduce.8
  343.4 23.4 reduce-scatter.9
  390.8 23.6 reduce-scatter.11
  445.4 21.6 reduce-scatter.13
  471.4 110.5 all-reduce.10
where the time goes:
time: 595 us; the launch traced here: 593 us
  local copies, waits for them, and re-layouts  284 us (48%)
  blocking collectives  136 us (23%)
  waiting for transfers between devices  115 us (19%)
  matrix products  25.7 us (4%)
  between operations  15.3 us (3%)
  starting transfers between devices  9.3 us (2%)
  other arithmetic  7.83 us (1%)
    gather x2, local copies, waits for them, and re-layouts, bias_rows(): return offsets[:, lookup]  236 us
    psum x1, waiting for transfers between devices, body(): lax.psum((grad_query, grad_key, grad_value, grad_out, table_grad, router_...  67.9 us
    psum x1, blocking collectives, body(): lax.psum((grad_query, grad_key, grad_value, grad_out, table_grad, router_...  39.1 us
    psum x1, waiting for transfers between devices, body(): resid_one = x_float + lax.psum(attn_partial, 'mp')  34.7 us
    all_gather x2, blocking collectives, send_rows(): arrived = lax.all_gather(arrived, 'mp', axis=2, tiled=True)  27 us
    all_to_all x2, blocking collectives, send_rows(): lax.all_to_all(buffer, 'expert', split_axis=0, concat_axis=0, tiled=True)  24.5 us
    unnamed x151, local copies, waits for them, and re-layouts  23.9 us
    all_gather x2, blocking collectives, whole_rows(): return lax.all_gather(share_rows, 'mp', axis=1, tiled=True)  12.7 us
  transfers between devices with their start and end apart: 7, of which 4 were waited for; matrix products, arithmetic and copies ran while one was open for 7% of the time, Pallas kernels for 0%

commit v1 on v0

v1 whole, which is shorter than its diff:
```python
import functools

import jax
import jax.numpy as jnp
from jax import lax
from jax.experimental import pallas as pl
from jax.experimental.pallas import tpu as pltpu
from jax.sharding import PartitionSpec as P

HEAD_DIM = 64
EPSILON = 1e-06
MESH = pl.DeviceIdType.MESH
F32 = jnp.float32
BF16 = jnp.bfloat16


def nn(left, right):
    return lax.dot_general(left, right, (((1,), (0,)), ((), ())), preferred_element_type=F32)


def nt(left, right):
    return lax.dot_general(left, right, (((1,), (1,)), ((), ())), preferred_element_type=F32)


def tn(left, right):
    return lax.dot_general(left, right, (((0,), (0,)), ((), ())), preferred_element_type=F32)


def kernel(
    n_exp,
    cap,
    x_in,
    cot_in,
    small_in,
    wq,
    wk,
    wv,
    wo_in,
    table,
    w_in,
    w_eo,
    routes,
    slots,
    bucket_rev,
    mixed_out,
    gtok_out,
    ggain1_out,
    ggain2_out,
    gq_out,
    gk_out,
    gv_out,
    gout_out,
    gtable_out,
    grouter_out,
    rows_out,
    hidden_out,
    dpre_out,
    x_all,
    cot_all,
    small_all,
    wo_all,
    att_own,
    att_all,
    n1_s,
    r1_s,
    q_s,
    k_s,
    v_s,
    probs_s,
    pair_s,
    disp_s,
    part_s,
    rs_s,
    home_send,
    home_s,
    ret_own,
    ret_all,
    gg2_s,
    grouter_s,
    dres_s,
    dq_s,
    dk_s,
    dv_s,
    dn_send,
    dn_recv,
    s1,
    r1,
    s2,
    r2,
    s3,
    r3,
    s4,
    r4,
    s5,
    r5,
    s6,
    r6,
    s7,
    r7,
    s8,
    r8,
):
    e = lax.axis_index("expert")
    m = lax.axis_index("mp")
    n_mp = 4
    cs, length = x_in.shape
    width = cs * n_mp
    half = width // 2
    rows = n_exp * cap
    heads = cs // HEAD_DIM
    factor = HEAD_DIM ** (-0.5)
    quarter = lax.rem(m, 2) * 2 + m // 2

    barrier = pltpu.get_barrier_semaphore()
    for d in range(1, n_mp):
        pl.semaphore_signal(
            barrier, inc=1, device_id=(e, lax.rem(m + d, n_mp)), device_id_type=MESH
        )

    def greet(d, carry):
        pl.semaphore_signal(
            barrier, inc=1, device_id=(lax.rem(e + d, n_exp), m), device_id_type=MESH
        )
        return carry

    lax.fori_loop(1, n_exp, greet, 0)
    pl.semaphore_wait(barrier, n_mp - 1 + n_exp - 1)

    def to_mp(src, dst, send, recv, d):
        return pltpu.make_async_remote_copy(
            src_ref=src,
            dst_ref=dst,
            send_sem=send,
            recv_sem=recv,
            device_id=(e, lax.rem(m + d, n_mp)),
            device_id_type=MESH,
        )

    def to_expert(src, dst, send, recv, d):
        return pltpu.make_async_remote_copy(
            src_ref=src,
            dst_ref=dst,
            send_sem=send,
            recv_sem=recv,
            device_id=(lax.rem(e + d, n_exp), m),
            device_id_type=MESH,
        )

    own = pl.ds(pl.multiple_of(m * cs, cs), cs)
    gathers = []
    for k, (src, full) in enumerate(
        ((x_in, x_all), (small_in, small_all), (wo_in, wo_all), (cot_in, cot_all))
    ):
        for d in range(1, n_mp):
            copy = to_mp(src, full.at[own], s1.at[k, d], r1.at[k, d], d)
            copy.start()
            gathers.append(copy)
    x_all[own] = x_in[...]
    small_all[own] = small_in[...]
    wo_all[own] = wo_in[...]
    cot_all[own] = cot_in[...]

    buckets = table.shape[0]
    onehot = (
        lax.broadcasted_iota(jnp.int32, (buckets, 2 * length), 0) == bucket_rev[...]
    ).astype(F32)
    table_f = table[...].astype(F32)

    def head_bias(h):
        line = jnp.sum(table_f[:, h : h + 1] * onehot, axis=0, keepdims=True)
        spread = jnp.broadcast_to(line, (length, 2 * length))
        turned = pltpu.roll(spread, length + 1, 1, stride=1, stride_axis=0)
        return turned[:, :length]

    for h in range(heads):
        probs_s[h] = head_bias(h)

    for copy in gathers[:6]:
        copy.wait()
    gain1 = small_all[:, n_exp : n_exp + 1].astype(F32)
    gain2 = small_all[:, n_exp + 1 : n_exp + 2].astype(F32)
    xf = x_all[...].astype(F32)
    inv_one = lax.rsqrt(jnp.sum(xf * xf, axis=0, keepdims=True) / width + EPSILON)
    n1_s[...] = (xf * inv_one * gain1).astype(BF16)
    q_s[...] = tn(wq[...], n1_s[...]).astype(BF16)
    k_s[...] = tn(wk[...], n1_s[...]).astype(BF16)
    v_s[...] = tn(wv[...], n1_s[...]).astype(BF16)
    for h in range(heads):
        hs = pl.ds(h * HEAD_DIM, HEAD_DIM)
        scores = tn(k_s[hs], q_s[hs]) * factor + probs_s[h]
        raised = jnp.exp(scores - jnp.max(scores, axis=0, keepdims=True))
        probs = raised / jnp.sum(raised, axis=0, keepdims=True)
        probs_s[h] = probs
        att_own[hs] = nn(v_s[hs], probs.astype(BF16)).astype(BF16)

    gathers2 = []
    for d in range(1, n_mp):
        copy = to_mp(att_own, att_all.at[own], s2.at[d], r2.at[d], d)
        copy.start()
        gathers2.append(copy)
    att_all[own] = att_own[...]
    for copy in gathers[6:] + gathers2:
        copy.wait()

    resid = x_all[...].astype(F32) + tn(wo_all[...], att_all[...])
    r1_s[...] = resid
    inv_two = lax.rsqrt(jnp.sum(resid * resid, axis=0, keepdims=True) / width + EPSILON)
    n2 = (resid * inv_two * gain2).astype(BF16)
    router = small_all[:, :n_exp]
    logits = tn(router, n2)
    lifted = jnp.exp(logits - jnp.max(logits, axis=0, keepdims=True))
    router_probs = lifted / jnp.sum(lifted, axis=0, keepdims=True)
    picked = (
        lax.broadcasted_iota(jnp.int32, (n_exp, length), 0) == routes[...]
    ).astype(F32)
    gate = jnp.sum(router_probs * picked, axis=0, keepdims=True)
    d_ret = (gate * cot_all[...].astype(F32)).astype(BF16)
    pair_s[0] = n2[:half]
    pair_s[1] = n2[half:]
    pair_s[2] = d_ret[:half]
    pair_s[3] = d_ret[half:]
    target = routes[...] * cap + slots[...]
    place = (lax.broadcasted_iota(jnp.int32, (rows, length), 0) == target).astype(F32).astype(BF16)
    disp_s[...] = nt(place, pair_s[quarter]).astype(BF16).reshape(n_exp, cap, half)

    def dispatch(d):
        return to_expert(
            disp_s.at[lax.rem(e + d, n_exp)],
            rows_out.at[quarter, e],
            s3.at[d],
            r3.at[d],
            d,
        )

    def forward(d, j):
        block = lax.rem(e - d + n_exp, n_exp)
        return to_mp(
            rows_out.at[quarter, block],
            rows_out.at[quarter, block],
            s4.at[j, d],
            r4.at[j, d],
            j,
        )

    def send_loop(d, carry):
        dispatch(d).start()
        return carry

    lax.fori_loop(1, n_exp, send_loop, 0)
    rows_out[quarter, e] = disp_s[e]
    for j in range(1, n_mp):
        forward(0, j).start()

    def pass_loop(d, carry):
        dispatch(d).wait_recv()
        for j in range(1, n_mp):
            forward(d, j).start()
        return carry

    lax.fori_loop(1, n_exp, pass_loop, 0)

    def settle(d, carry):
        for j in range(1, n_mp):
            forward(d, j).wait()
        return carry

    lax.fori_loop(0, n_exp, settle, 0)

    def settle_sends(d, carry):
        dispatch(d).wait_send()
        return carry

    lax.fori_loop(1, n_exp, settle_sends, 0)

    in_a = rows_out[0].reshape(rows, half)
    in_b = rows_out[1].reshape(rows, half)
    pre = nn(in_a, w_in[:half]) + nn(in_b, w_in[half:])
    inner = 0.7978845608 * (pre + 0.044715 * pre * pre * pre)
    bent = jnp.tanh(inner)
    hidden_out[...] = (0.5 * pre * (1.0 + bent)).astype(BF16)
    slope = 0.5 * (1.0 + bent) + 0.5 * pre * (1.0 - bent * bent) * 0.7978845608 * (
        1.0 + 3.0 * 0.044715 * pre * pre
    )
    d_hidden = nt(rows_out[2].reshape(rows, half), w_eo[:, :half]) + nt(
        rows_out[3].reshape(rows, half), w_eo[:, half:]
    )
    dpre_out[...] = (d_hidden * slope).astype(BF16)
    part_s[0] = nn(hidden_out[...], w_eo[:, :half]).astype(BF16)
    part_s[1] = nn(hidden_out[...], w_eo[:, half:]).astype(BF16)
    part_s[2] = nt(dpre_out[...], w_in[:half]).astype(BF16)
    part_s[3] = nt(dpre_out[...], w_in[half:]).astype(BF16)

    sums = []
    for d in range(1, n_mp):
        peer = lax.rem(m + d, n_mp)
        peer_quarter = lax.rem(peer, 2) * 2 + peer // 2
        copy = to_mp(part_s.at[peer_quarter], rs_s.at[d], s5.at[d], r5.at[d], d)
        copy.start()
        sums.append(copy)
    for copy in sums:
        copy.wait()
    total = part_s[quarter].astype(F32)
    for d in range(1, n_mp):
        total = total + rs_s[d].astype(F32)
    home_send[...] = total.astype(BF16).reshape(n_exp, cap, half)

    def homeward(d):
        return to_expert(
            home_send.at[lax.rem(e + d, n_exp)], home_s.at[e], s6.at[d], r6.at[d], d
        )

    def home_start(d, carry):
        homeward(d).start()
        return carry

    def home_wait(d, carry):
        homeward(d).wait()
        return carry

    lax.fori_loop(1, n_exp, home_start, 0)
    home_s[e] = home_send[e]
    lax.fori_loop(1, n_exp, home_wait, 0)
    ret_own[...] = tn(home_s[...].reshape(rows, half), place).astype(BF16)
    spot = pl.ds(pl.multiple_of(quarter * half, half), half)
    backs = []
    for d in range(1, n_mp):
        copy = to_mp(ret_own, ret_all.at[spot], s7.at[d], r7.at[d], d)
        copy.start()
        backs.append(copy)
    ret_all[spot] = ret_own[...]
    for copy in backs:
        copy.wait()

    mixed_out[...] = (r1_s[own] + gate * ret_all[own].astype(F32)).astype(BF16)
    cot_f = cot_all[...].astype(F32)
    d_gate = jnp.sum(cot_f * ret_all[:width].astype(F32), axis=0, keepdims=True)
    d_logits = (d_gate * gate * (picked - router_probs)).astype(BF16)
    resid = r1_s[...]
    hat_two = resid * inv_two
    n2_again = (hat_two * gain2).astype(BF16)
    grouter_s[...] = nt(n2_again, d_logits)
    d_n2 = ret_all[width:].astype(F32) + nn(router, d_logits)
    gg2_s[...] = jnp.sum(d_n2 * hat_two, axis=1, keepdims=True)
    u_two = d_n2 * gain2
    d_resid = cot_f + inv_two * (
        u_two - hat_two * (jnp.sum(u_two * hat_two, axis=0, keepdims=True) / width)
    )
    dres_s[...] = d_resid
    grouter_out[...] = grouter_s[own]
    ggain2_out[...] = gg2_s[own]
    d_attn = d_resid.astype(BF16)
    gout_out[...] = nt(att_own[...], d_attn)
    d_att = nn(wo_in[...], d_attn).astype(BF16)

    flip = (
        lax.broadcasted_iota(jnp.int32, (length, length), 0)
        + lax.broadcasted_iota(jnp.int32, (length, length), 1)
        == length - 1
    ).astype(F32).astype(BF16)
    for h in range(heads):
        hs = pl.ds(h * HEAD_DIM, HEAD_DIM)
        d_h = d_att[h * HEAD_DIM : (h + 1) * HEAD_DIM]
        probs = probs_s[h]
        d_probs = tn(v_s[hs], d_h)
        inner_sum = jnp.sum(d_probs * probs, axis=0, keepdims=True)
        d_scores = (probs * (d_probs - inner_sum)).astype(BF16)
        dq_s[hs] = (nn(k_s[hs], d_scores) * factor).astype(BF16)
        dk_s[hs] = (nt(q_s[hs], d_scores) * factor).astype(BF16)
        dv_s[hs] = nt(d_h, probs.astype(BF16)).astype(BF16)
        flipped = nn(flip, d_scores)
        padded = jnp.concatenate([flipped, jnp.zeros_like(flipped)], axis=1)
        turned = pltpu.roll(padded, 0, 1, stride=1, stride_axis=0)
        line = jnp.sum(turned, axis=0, keepdims=True)
        gtable_out[:, h : h + 1] = jnp.sum(onehot * line, axis=1, keepdims=True)

    d_n1 = nn(wq[...], dq_s[...]) + nn(wk[...], dk_s[...]) + nn(wv[...], dv_s[...])
    xf = x_all[...].astype(F32)
    stat = jnp.sum(d_n1 * gain1 * xf * inv_one, axis=0, keepdims=True)
    for p in range(n_mp):
        dn_send[p, :cs] = d_n1[p * cs : (p + 1) * cs].astype(BF16)
        dn_send[p, cs:] = jnp.broadcast_to(stat, (16, length)).astype(BF16)
    lasts = []
    for d in range(1, n_mp):
        copy = to_mp(
            dn_send.at[lax.rem(m + d, n_mp)], dn_recv.at[d], s8.at[d], r8.at[d], d
        )
        copy.start()
        lasts.append(copy)
    gq_out[...] = nt(n1_s[...], dq_s[...])
    gk_out[...] = nt(n1_s[...], dk_s[...])
    gv_out[...] = nt(n1_s[...], dv_s[...])
    for copy in lasts:
        copy.wait()
    both = dn_send[m].astype(F32)
    for d in range(1, n_mp):
        both = both + dn_recv[d].astype(F32)
    d_own = both[:cs]
    mean_own = both[cs : cs + 1] / width
    hat_one = x_in[...].astype(F32) * inv_one
    gain1_own = small_in[:, n_exp : n_exp + 1].astype(F32)
    gtok_out[...] = dres_s[own] + inv_one * (d_own * gain1_own - hat_one * mean_own)
    ggain1_out[...] = jnp.sum(d_own * hat_one, axis=1, keepdims=True)


def body(
    n_exp,
    tokens,
    gain_one,
    gain_two,
    w_query,
    w_key,
    w_value,
    w_out,
    bias_table,
    w_router,
    w_in,
    w_exp_out,
    cotangent,
    routes,
    slot_index,
    bucket,
):
    length, cs = tokens.shape
    n_mp = 4
    width = cs * n_mp
    half = width // 2
    capacity = max(2, (length * 9 + 8 * n_exp - 1) // (8 * n_exp))
    cap = -(-capacity // 16) * 16
    rows = n_exp * cap
    hid = w_in.shape[2]
    heads = cs // HEAD_DIM
    buckets = bias_table.shape[0]
    small = jnp.concatenate([w_router, gain_one[:, None], gain_two[:, None]], axis=1)
    bucket_rev = jnp.concatenate(
        [bucket[::-1], jnp.full((1,), -1, jnp.int32)]
    )[None, :]
    sds = jax.ShapeDtypeStruct
    vm = pltpu.VMEM
    dma = pltpu.SemaphoreType.DMA
    outs = pl.pallas_call(
        functools.partial(kernel, n_exp, cap),
        out_shape=(
            sds((cs, length), BF16),
            sds((cs, length), F32),
            sds((cs, 1), F32),
            sds((cs, 1), F32),
            sds((width, cs), F32),
            sds((width, cs), F32),
            sds((width, cs), F32),
            sds((cs, width), F32),
            sds((buckets, heads), F32),
            sds((cs, n_exp), F32),
            sds((4, n_exp, cap, half), BF16),
            sds((rows, hid), BF16),
            sds((rows, hid), BF16),
        ),
        in_specs=[pl.BlockSpec(memory_space=vm)] * 13,
        out_specs=tuple([pl.BlockSpec(memory_space=vm)] * 13),
        scratch_shapes=[
            vm((width, length), BF16),
            vm((width, length), BF16),
            vm((width, n_exp + 2), BF16),
            vm((width, width), BF16),
            vm((cs, length), BF16),
            vm((width, length), BF16),
            vm((width, length), BF16),
            vm((width, length), F32),
            vm((cs, length), BF16),
            vm((cs, length), BF16),
            vm((cs, length), BF16),
            vm((heads, length, length), F32),
            vm((4, half, length), BF16),
            vm((n_exp, cap, half), BF16),
            vm((4, rows, half), BF16),
            vm((4, rows, half), BF16),
            vm((n_exp, cap, half), BF16),
            vm((n_exp, cap, half), BF16),
            vm((half, length), BF16),
            vm((4 * half, length), BF16),
            vm((width, 1), F32),
            vm((width, n_exp), F32),
            vm((width, length), F32),
            vm((cs, length), BF16),
            vm((cs, length), BF16),
            vm((cs, length), BF16),
            vm((4, cs + 16, length), BF16),
            vm((4, cs + 16, length), BF16),
            dma((4, 4)),
            dma((4, 4)),
            dma((4,)),
            dma((4,)),
            dma((n_exp,)),
            dma((n_exp,)),
            dma((4, n_exp)),
            dma((4, n_exp)),
            dma((4,)),
            dma((4,)),
            dma((n_exp,)),
            dma((n_exp,)),
            dma((4,)),
            dma((4,)),
            dma((4,)),
            dma((4,)),
        ],
        compiler_params=pltpu.CompilerParams(
            collective_id=0, has_side_effects=True, vmem_limit_bytes=60 * 2**20
        ),
    )(
        tokens.T,
        cotangent.T,
        small,
        w_query,
        w_key,
        w_value,
        w_out,
        bias_table,
        w_in[0],
        w_exp_out[0],
        routes[None, :],
        slot_index[None, :],
        bucket_rev,
    )
    mixed, gtok, gg1, gg2, gq, gk, gv, gout, gtable, grouter, blocks, hidden, d_pre = outs
    flat = blocks.reshape(4, rows, half)
    grad_in = jnp.einsum("hsd,sf->hdf", flat[:2], d_pre, preferred_element_type=F32).reshape(
        width, hid
    )
    d_rows = jnp.concatenate([flat[2], flat[3]], axis=1)
    grad_eo = jnp.einsum("sf,sd->fd", hidden, d_rows, preferred_element_type=F32)
    summed = lax.psum((gq, gk, gv, gout, gtable, grouter, gg1[:, 0], gg2[:, 0]), "expert")
    return (
        mixed.T,
        gtok.T,
        summed[6],
        summed[7],
        summed[0],
        summed[1],
        summed[2],
        summed[3],
        summed[4],
        summed[5],
        grad_in[None],
        grad_eo[None],
    )


def solution(mesh):
    return jax.shard_map(
        functools.partial(body, mesh.shape["expert"]),
        mesh=mesh,
        in_specs=(
            P("expert", "mp"),
            P("mp"),
            P("mp"),
            P(None, "mp"),
            P(None, "mp"),
            P(None, "mp"),
            P("mp", None),
            P(None, "mp"),
            P("mp", None),
            P("expert", None, "mp"),
            P("expert", "mp", None),
            P("expert", "mp"),
            P("expert"),
            P("expert"),
            P(),
        ),
        out_specs=(
            P("expert", "mp"),
            P("expert", "mp"),
            P("mp"),
            P("mp"),
            P(None, "mp"),
            P(None, "mp"),
            P(None, "mp"),
            P("mp", None),
            P(None, "mp"),
            P("mp", None),
            P("expert", None, "mp"),
            P("expert", "mp", None),
        ),
        check_vma=False,
    )
```

time: 595 us -> 258 us (0.43)
  local copies, waits for them, and re-layouts: 284 us -> 17.5 us
  Pallas kernels: 0 us -> 97.8 us
  blocking collectives: 136 us -> 43.4 us
  waiting for transfers between devices: 115 us -> 78.8 us
  matrix products: 25.7 us -> 4.38 us
  starting transfers between devices: 9.3 us -> 0.04 us
  other arithmetic: 7.83 us -> 1.56 us
    gather x6 -> x0, local copies, waits for them, and re-layouts: 239 us -> none  [the longest x2 236 us: bias_rows(): return offsets[:, lookup]]
    pallas_call x0 -> x1, Pallas kernels: none -> 97.8 us  [body(): pl.pallas_call(functools.partial(kernel, n_exp, cap), out_shape=(sds((cs,...]
    all_gather x7 -> x0, blocking collectives: 59.8 us -> none  [the longest x2 27 us: send_rows(): arrived = lax.all_gather(arrived, 'mp', axis=2, tiled=True)]
    all_to_all x2 -> x0, blocking collectives: 24.5 us -> none  [send_rows(): lax.all_to_all(buffer, 'expert', split_axis=0, concat_axis=0, tiled=True)]
    psum x2 -> x1, waiting for transfers between devices: 103 us -> 78.7 us  [body(): lax.psum((gq, gk, gv, gout, gtable, grouter, gg1[:, 0], gg2[:, 0]), 'expe...]
    dot_general x27 -> x2, matrix products: 22 us -> 4.38 us  [the longest x1 2.21 us: body(): jnp.einsum('sf,sd->fd', hidden, d_rows, preferred_element_type=F32)]
    reshape x9 -> x0, local copies, waits for them, and re-layouts: 12.4 us -> none  [the longest x2 6.44 us: send_rows(): return arrived.reshape(experts * capacity, arrived.shape[2])]
    unnamed x8 -> x1, waiting for transfers between devices: 12.4 us -> 0.02 us
  transfers between devices with their start and end apart: 7 -> 1, of which waited for: 4 -> 1; matrix products, arithmetic and copies ran while one was open for 7% -> 2% of each run, Pallas kernels for 0% -> 0%
where the time goes in v1:
time: 258 us
  Pallas kernels  97.8 us (38%)
  waiting for transfers between devices  78.8 us (31%)
  blocking collectives  43.4 us (17%)
  local copies, waits for them, and re-layouts  17.5 us (7%)
  between operations  14.2 us (6%)
  matrix products  4.38 us (2%)
    pallas_call x1, Pallas kernels, body(): pl.pallas_call(functools.partial(kernel, n_exp, cap), out_shape=(sds((cs,...  97.8 us
    psum x1, waiting for transfers between devices, body(): lax.psum((gq, gk, gv, gout, gtable, grouter, gg1[:, 0], gg2[:, 0]), 'expe...  78.7 us
    psum x1, blocking collectives, body(): lax.psum((gq, gk, gv, gout, gtable, grouter, gg1[:, 0], gg2[:, 0]), 'expe...  43.4 us
    unnamed x44, local copies, waits for them, and re-layouts  15 us
  transfers between devices with their start and end apart: 1, of which 1 were waited for; matrix products, arithmetic and copies ran while one was open for 2% of the time, Pallas kernels for 0%

profile of v1, /device:TPU:0, one launch (start us, length us, event | category | flops | bytes accessed | tf_op | source)
XLA Modules:
  0.0 257.7 jit_solution(14218070036867726205)
XLA Ops:
  7.2 0.0 copy-start.6
  7.2 0.0 copy-start.14
  7.2 0.0 copy-start.13
  7.2 0.0 all-reduce.4.cloned.1.call-start
  7.3 0.7 broadcast_in_dim.19
  8.0 0.7 broadcast_in_dim.18
  8.6 0.7 pad_maximum_fusion
  9.3 0.7 copy.50.small_in
  10.0 1.9 copy.51.wq
  11.9 1.9 copy.52.wk
  13.8 0.0 copy-done.6
  13.8 0.9 copy.53.wv
  14.7 0.0 copy-done.14
  14.7 0.7 copy.54.table
  15.4 0.0 copy-done.13
  15.4 0.1 reverse
  15.5 0.1 slice.18
  15.6 0.7 pad_add_fusion
  16.3 97.8 %shard_map.238 = (bf16[192,256]{1,0:T(8,128)(2,1)}, f32[192,256]{1,0:T(8,128)}, f32[192,1]{1,0:T(8,128)}, f32[192,1]{1,0:T(8,128)}, f32[768,192]{1,0:T(8,128)}, ...) custom-call(bf16[192,256]{1,0:T(8,128)(2,1)} %bitcast.31, ...), custom_call_target="tpu_custom_call" | custom-call | tf_op jit(solution)/shard_map/pallas_call | solution.py:440
  114.1 0.0 copy-start.11
  114.1 0.0 copy-start.10
  114.1 0.0 copy-start.9
  114.1 0.0 copy-start.12
  114.1 0.0 copy-start
  114.1 0.0 all-reduce.4.cloned.1.call-update
  114.2 0.8 copy-done.11
  115.0 0.1 reduce
  115.1 0.0 copy-done.10
  115.1 0.1 reduce.1
  115.2 0.0 copy-done.9
  115.2 0.0 copy-done.12
  115.2 43.4 %all-reduce = (f32[192]{0:T(256)}, f32[192]{0:T(256)}, f32[32,3]{1,0:T(8,128)S(1)}, f32[192,8]{1,0:T(8,128)S(1)}) all-reduce(f32[192]{0:T(256)S(1)} %reduce, f32[192]{0:T(256)S(1)} %reduce.1, f32[32,3]{1,0:T(8,128)S(1)} %copy-done.12, f32[192,8]{1,0:T(8,128)S(1)} %copy-done.9), channel_id=1, replica_groups=mesh['expert'=8,'mp'=4] {'expert'}, use_global_device_ids=true, to_apply=%region_0.0 | all-reduce | flops 2016 | bytes 16128 | tf_op jit(solution)/shard_map/psum | solution.py:530
  158.7 0.7 copy.59
  159.3 0.7 copy.60
  160.0 0.0 copy-done
  160.0 0.1 slice.14
  160.1 0.3 copy.55
  160.4 0.1 fusion.4
  160.4 0.7 copy-done.4
  161.1 2.2 convolution_bitcast_fusion
  163.3 2.2 convolution_bitcast_fusion.1
  165.5 78.7 %all-reduce.4.cloned.1.call-done = (f32[768,192]{1,0:T(8,128)}, f32[768,192]{1,0:T(8,128)}, f32[768,192]{1,0:T(8,128)}, f32[192,768]{1,0:T(8,128)}) async-done(((f32[768,192]{1,0:T(8,128)}, f32[768,192]{1,0:T(8,128)}, f32[768,192]{1,0:T(8,128)}, f32[192,768]{1,0:T(8,128)}), (f32[768,192]{1,0:T(8,128)}, f32[768,192]{1,0:T(8,128)}, f32[768,192]{1,0:T(8,128)}, ...) | async-done | bytes 2359312 | tf_op jit(solution)/shard_map/psum | solution.py:530
  244.3 2.3 copy.56
  246.6 1.1 copy.57
  247.7 1.1 copy.58
  248.7 0.6 copy.68
  249.4 0.7 copy.69
  250.1 0.8 copy.70
  (13 shorter events, 0.0 us)
Async XLA Ops:
  7.2 6.6 %copy-start.6 = (bf16[768,192]{0,1:T(8,128)(2,1)S(1)}, bf16[768,192]{0,1:T(8,128)(2,1)}, u32[]{:S(2)}) copy-start(bf16[768,192]{0,1:T(8,128)(2,1)} %param.20) | copy-start | bytes 884740
  7.2 7.5 %copy-start.14 = (bf16[32,3]{0,1:T(4,128)(2,1)S(1)}, bf16[32,3]{0,1:T(4,128)(2,1)}, u32[]{:S(2)}) copy-start(bf16[32,3]{0,1:T(4,128)(2,1)} %param.22) | copy-start | bytes 580
  7.2 8.2 %copy-start.13 = (s32[511]{0:T(512)S(1)}, s32[511]{0:T(512)}, u32[]{:S(2)}) copy-start(s32[511]{0:T(512)} %param.29) | copy-start | bytes 6136
  7.2 237.0 %all-reduce.4.cloned.1.call-start = ((), (), s32[]{:S(2)}) async-start(), calls=%async_computation | async-start | bytes 5898240 | tf_op jit(solution)/shard_map/psum | solution.py:530
  114.1 0.9 copy-start.11
  114.1 1.0 copy-start.10
  114.1 1.1 copy-start.9
  114.1 1.1 copy-start.12
  114.1 45.9 %copy-start = (bf16[4,8,48,384]{3,2,1,0:T(8,128)(2,1)S(1)}, bf16[4,8,48,384]{3,2,1,0:T(8,128)(2,1)}, u32[]{:S(2)}) copy-start(bf16[4,8,48,384]{3,2,1,0:T(8,128)(2,1)} %get-tuple-element.35) | copy-start | bytes 3538948
  160.1 1.1 copy-start.4
  161.1 2.2 copy-start.3
  244.3 2.3 copy-start.2
  244.3 3.4 %copy-start.1 = (f32[768,192]{1,0:T(8,128)S(1)}, f32[768,192]{1,0:T(8,128)}, u32[]{:S(2)}) copy-start(f32[768,192]{1,0:T(8,128)} %get-tuple-element.80) | copy-start | bytes 1769476
  246.6 2.1 copy-start.8
  246.6 2.8 %copy-start.7 = (f32[192,256]{1,0:T(8,128)S(1)}, f32[192,256]{1,0:T(8,128)}, u32[]{:S(2)}) copy-start(f32[192,256]{1,0:T(8,128)} %get-tuple-element.26) | copy-start | bytes 589828
  247.7 2.4 copy-start.5
Sparse Core Ops, SparseCore 0:
  114.3 129.9 all-reduce.3

commit v2 on v1

--- a/solution.py
+++ b/solution.py
@@ -29,6 +29,7 @@
 def kernel(
     n_exp,
     cap,
+    n_x,
     x_in,
     cot_in,
     small_in,
@@ -44,14 +45,8 @@
     bucket_rev,
     mixed_out,
     gtok_out,
-    ggain1_out,
-    ggain2_out,
-    gq_out,
-    gk_out,
-    gv_out,
-    gout_out,
-    gtable_out,
-    grouter_out,
+    grads_out,
+    tiny_out,
     rows_out,
     hidden_out,
     dpre_out,
@@ -75,14 +70,26 @@
     home_s,
     ret_own,
     ret_all,
-    gg2_s,
-    grouter_s,
     dres_s,
+    turn_s,
     dq_s,
     dk_s,
     dv_s,
+    rs_b,
+    rs_c,
     dn_send,
     dn_recv,
+    dn_b,
+    dn_c,
+    g_send,
+    g_x,
+    g_part,
+    g_z,
+    g_all,
+    tiny_s,
+    tiny_x,
+    tiny_b,
+    tiny_z,
     s1,
     r1,
     s2,
@@ -99,6 +106,10 @@
     r7,
     s8,
     r8,
+    s9,
+    r9,
+    s10,
+    r10,
 ):
     e = lax.axis_index("expert")
     m = lax.axis_index("mp")
@@ -109,7 +120,17 @@
     rows = n_exp * cap
     heads = cs // HEAD_DIM
     factor = HEAD_DIM ** (-0.5)
-    quarter = lax.rem(m, 2) * 2 + m // 2
+    fuse = n_exp == 8 and n_x == 2
+    core = lax.rem(m, 2)
+    side = m // 2
+    quarter = core * 2 + side
+    sibling = m + 1 - 2 * core
+    across = lax.rem(m + 2, n_mp)
+    far = sibling + 2 - 4 * (sibling // 2)
+    across_quarter = core * 2 + 1 - side
+    z = e // n_x
+    n_z = n_exp // n_x
+    x = lax.rem(e, n_x)
 
     barrier = pltpu.get_barrier_semaphore()
     for d in range(1, n_mp):
@@ -126,15 +147,35 @@
     lax.fori_loop(1, n_exp, greet, 0)
     pl.semaphore_wait(barrier, n_mp - 1 + n_exp - 1)
 
-    def to_mp(src, dst, send, recv, d):
+    def to_mp(src, dst, send, recv, peer):
         return pltpu.make_async_remote_copy(
             src_ref=src,
             dst_ref=dst,
             send_sem=send,
             recv_sem=recv,
-            device_id=(e, lax.rem(m + d, n_mp)),
+            device_id=(e, peer),
             device_id_type=MESH,
         )
+
+    def spread(src, full, place_of, send, recv):
+        near = to_mp(src, full.at[place_of(m)], send.at[1], recv.at[1], sibling)
+        over = to_mp(src, full.at[place_of(m)], send.at[2], recv.at[2], across)
+        theirs = full.at[place_of(across)]
+        relay = to_mp(theirs, theirs, send.at[3], recv.at[3], sibling)
+        return over, near, relay
+
+    def begin(trio):
+        trio[0].start()
+        trio[1].start()
+
+    def pass_on(trio):
+        trio[0].wait_recv()
+        trio[2].start()
+
+    def finish(trio):
+        trio[0].wait_send()
+        trio[1].wait()
+        trio[2].wait()
 
     def to_expert(src, dst, send, recv, d):
         return pltpu.make_async_remote_copy(
@@ -146,17 +187,20 @@
             device_id_type=MESH,
         )
 
-    own = pl.ds(pl.multiple_of(m * cs, cs), cs)
-    gathers = []
-    for k, (src, full) in enumerate(
-        ((x_in, x_all), (small_in, small_all), (wo_in, wo_all), (cot_in, cot_all))
-    ):
-        for d in range(1, n_mp):
-            copy = to_mp(src, full.at[own], s1.at[k, d], r1.at[k, d], d)
-            copy.start()
-            gathers.append(copy)
+    def band(p):
+        return pl.ds(pl.multiple_of(p * cs, cs), cs)
+
+    own = band(m)
+    small_all[m] = small_in[...]
+    trios = [
+        spread(x_in, x_all, band, s1.at[0], r1.at[0]),
+        spread(small_in, small_all, lambda p: p, s1.at[1], r1.at[1]),
+        spread(wo_in, wo_all, band, s1.at[2], r1.at[2]),
+        spread(cot_in, cot_all, band, s1.at[3], r1.at[3]),
+    ]
+    for trio in trios:
+        begin(trio)
     x_all[own] = x_in[...]
-    small_all[own] = small_in[...]
     wo_all[own] = wo_in[...]
     cot_all[own] = cot_in[...]
 
@@ -175,16 +219,25 @@
     for h in range(heads):
         probs_s[h] = head_bias(h)
 
-    for copy in gathers[:6]:
-        copy.wait()
-    gain1 = small_all[:, n_exp : n_exp + 1].astype(F32)
-    gain2 = small_all[:, n_exp + 1 : n_exp + 2].astype(F32)
+    for trio in trios[:2]:
+        pass_on(trio)
+    for trio in trios[:2]:
+        finish(trio)
+    n_small = small_in.shape[0]
+    unit = (
+        lax.broadcasted_iota(jnp.int32, (n_small, n_small), 0)
+        == lax.broadcasted_iota(jnp.int32, (n_small, n_small), 1)
+    ).astype(F32).astype(BF16)
+    for p in range(n_mp):
+        turn_s[p * cs : (p + 1) * cs] = tn(small_all[p], unit)
+    gain1 = turn_s[:, n_exp : n_exp + 1]
+    gain2 = turn_s[:, n_exp + 1 : n_exp + 2]
     xf = x_all[...].astype(F32)
     inv_one = lax.rsqrt(jnp.sum(xf * xf, axis=0, keepdims=True) / width + EPSILON)
     n1_s[...] = (xf * inv_one * gain1).astype(BF16)
-    q_s[...] = tn(wq[...], n1_s[...]).astype(BF16)
-    k_s[...] = tn(wk[...], n1_s[...]).astype(BF16)
-    v_s[...] = tn(wv[...], n1_s[...]).astype(BF16)
+    q_s[...] = nn(wq[...], n1_s[...]).astype(BF16)
+    k_s[...] = nn(wk[...], n1_s[...]).astype(BF16)
+    v_s[...] = nn(wv[...], n1_s[...]).astype(BF16)
     for h in range(heads):
         hs = pl.ds(h * HEAD_DIM, HEAD_DIM)
         scores = tn(k_s[hs], q_s[hs]) * factor + probs_s[h]
@@ -193,20 +246,20 @@
         probs_s[h] = probs
         att_own[hs] = nn(v_s[hs], probs.astype(BF16)).astype(BF16)
 
-    gathers2 = []
-    for d in range(1, n_mp):
-        copy = to_mp(att_own, att_all.at[own], s2.at[d], r2.at[d], d)
-        copy.start()
-        gathers2.append(copy)
+    att_trio = spread(att_own, att_all, band, s2, r2)
+    for trio in trios[2:]:
+        pass_on(trio)
+    begin(att_trio)
     att_all[own] = att_own[...]
-    for copy in gathers[6:] + gathers2:
-        copy.wait()
+    pass_on(att_trio)
+    for trio in trios[2:] + [att_trio]:
+        finish(trio)
 
     resid = x_all[...].astype(F32) + tn(wo_all[...], att_all[...])
     r1_s[...] = resid
     inv_two = lax.rsqrt(jnp.sum(resid * resid, axis=0, keepdims=True) / width + EPSILON)
     n2 = (resid * inv_two * gain2).astype(BF16)
-    router = small_all[:, :n_exp]
+    router = turn_s[:, :n_exp].astype(BF16)
     logits = tn(router, n2)
     lifted = jnp.exp(logits - jnp.max(logits, axis=0, keepdims=True))
     router_probs = lifted / jnp.sum(lifted, axis=0, keepdims=True)
@@ -232,14 +285,14 @@
             d,
         )
 
-    def forward(d, j):
+    def forward(d):
         block = lax.rem(e - d + n_exp, n_exp)
-        return to_mp(
-            rows_out.at[quarter, block],
-            rows_out.at[quarter, block],
-            s4.at[j, d],
-            r4.at[j, d],
-            j,
+        mine = rows_out.at[quarter, block]
+        theirs = rows_out.at[across_quarter, block]
+        return (
+            to_mp(mine, mine, s4.at[2, d], r4.at[2, d], across),
+            to_mp(mine, mine, s4.at[1, d], r4.at[1, d], sibling),
+            to_mp(theirs, theirs, s4.at[3, d], r4.at[3, d], sibling),
         )
 
     def send_loop(d, carry):
@@ -248,20 +301,23 @@
 
     lax.fori_loop(1, n_exp, send_loop, 0)
     rows_out[quarter, e] = disp_s[e]
-    for j in range(1, n_mp):
-        forward(0, j).start()
+    begin(forward(0))
 
     def pass_loop(d, carry):
         dispatch(d).wait_recv()
-        for j in range(1, n_mp):
-            forward(d, j).start()
+        begin(forward(d))
         return carry
 
     lax.fori_loop(1, n_exp, pass_loop, 0)
 
+    def relay_loop(d, carry):
+        pass_on(forward(d))
+        return carry
+
+    lax.fori_loop(0, n_exp, relay_loop, 0)
+
     def settle(d, carry):
-        for j in range(1, n_mp):
-            forward(d, j).wait()
+        finish(forward(d))
         return carry
 
     lax.fori_loop(0, n_exp, settle, 0)
@@ -290,18 +346,21 @@
     part_s[2] = nt(dpre_out[...], w_in[:half]).astype(BF16)
     part_s[3] = nt(dpre_out[...], w_in[half:]).astype(BF16)
 
-    sums = []
-    for d in range(1, n_mp):
-        peer = lax.rem(m + d, n_mp)
-        peer_quarter = lax.rem(peer, 2) * 2 + peer // 2
-        copy = to_mp(part_s.at[peer_quarter], rs_s.at[d], s5.at[d], r5.at[d], d)
-        copy.start()
-        sums.append(copy)
-    for copy in sums:
-        copy.wait()
-    total = part_s[quarter].astype(F32)
-    for d in range(1, n_mp):
-        total = total + rs_s[d].astype(F32)
+    def halve(parts, got, passing, last, send, recv):
+        first = to_mp(
+            parts.at[pl.ds(2 - 2 * core, 2)], got, send.at[1], recv.at[1], sibling
+        )
+        second = to_mp(passing, last, send.at[2], recv.at[2], across)
+        return first, second
+
+    first, second = halve(part_s, rs_s, rs_b, rs_c, s5, r5)
+    first.start()
+    first.wait()
+    rs_b[...] = (part_s[across_quarter].astype(F32) + rs_s[1 - side].astype(F32)).astype(BF16)
+    second.start()
+    total = part_s[quarter].astype(F32) + rs_s[side].astype(F32)
+    second.wait()
+    total = total + rs_c[...].astype(F32)
     home_send[...] = total.astype(BF16).reshape(n_exp, cap, half)
 
     def homeward(d):
@@ -321,16 +380,24 @@
     home_s[e] = home_send[e]
     lax.fori_loop(1, n_exp, home_wait, 0)
     ret_own[...] = tn(home_s[...].reshape(rows, half), place).astype(BF16)
-    spot = pl.ds(pl.multiple_of(quarter * half, half), half)
-    backs = []
-    for d in range(1, n_mp):
-        copy = to_mp(ret_own, ret_all.at[spot], s7.at[d], r7.at[d], d)
-        copy.start()
-        backs.append(copy)
-    ret_all[spot] = ret_own[...]
-    for copy in backs:
-        copy.wait()
-
+    def quarter_rows(p):
+        q = lax.rem(p, 2) * 2 + p // 2
+        return pl.ds(pl.multiple_of(q * half, half), half)
+
+    back_trio = spread(ret_own, ret_all, quarter_rows, s7, r7)
+    begin(back_trio)
+    ret_all[quarter_rows(m)] = ret_own[...]
+    pass_on(back_trio)
+    finish(back_trio)
+
+    ones = jnp.ones((8, length), F32).astype(BF16)
+
+    def lane_sums(values):
+        high = values.astype(BF16)
+        rest = (values - high.astype(F32)).astype(BF16)
+        return nt(ones[:, : values.shape[1]], high) + nt(ones[:, : values.shape[1]], rest)
+
+    tiny_s[...] = jnp.zeros_like(tiny_s)
     mixed_out[...] = (r1_s[own] + gate * ret_all[own].astype(F32)).astype(BF16)
     cot_f = cot_all[...].astype(F32)
     d_gate = jnp.sum(cot_f * ret_all[:width].astype(F32), axis=0, keepdims=True)
@@ -338,18 +405,88 @@
     resid = r1_s[...]
     hat_two = resid * inv_two
     n2_again = (hat_two * gain2).astype(BF16)
-    grouter_s[...] = nt(n2_again, d_logits)
+    tiny_s[:n_exp] = nt(d_logits, n2_again)
     d_n2 = ret_all[width:].astype(F32) + nn(router, d_logits)
-    gg2_s[...] = jnp.sum(d_n2 * hat_two, axis=1, keepdims=True)
+    tiny_s[n_exp : n_exp + 8] = lane_sums(d_n2 * hat_two)
     u_two = d_n2 * gain2
     d_resid = cot_f + inv_two * (
         u_two - hat_two * (jnp.sum(u_two * hat_two, axis=0, keepdims=True) / width)
     )
     dres_s[...] = d_resid
-    grouter_out[...] = grouter_s[own]
-    ggain2_out[...] = gg2_s[own]
     d_attn = d_resid.astype(BF16)
-    gout_out[...] = nt(att_own[...], d_attn)
+    lanes = width // n_x
+    n_rows = cs // n_z if fuse else cs
+    x_peer = n_x - 1 - x
+
+    def lane_band(k):
+        return pl.ds(pl.multiple_of(k * lanes, lanes), lanes)
+
+    def row_band(k):
+        return pl.ds(pl.multiple_of(k * n_rows, n_rows), n_rows)
+
+    def remote(src, dst, kind, i, d, where):
+        return pltpu.make_async_remote_copy(
+            src_ref=src,
+            dst_ref=dst,
+            send_sem=s9.at[kind, i, d],
+            recv_sem=r9.at[kind, i, d],
+            device_id=(where, m),
+            device_id_type=MESH,
+        )
+
+    def to_x(i):
+        return remote(
+            g_send.at[i, :, lane_band(x_peer)], g_x.at[i], 0, i, 0, z * n_x + x_peer
+        )
+
+    def to_z(i, d):
+        zp = lax.rem(z + d, n_z)
+        return remote(g_part.at[i, row_band(zp)], g_z.at[i, d], 1, i, d, zp * n_x + x)
+
+    def out_z(i, d):
+        zp = lax.rem(z + d, n_z)
+        spot = g_all.at[i, row_band(z), lane_band(x)]
+        return remote(spot, spot, 2, i, d, zp * n_x + x)
+
+    def out_x(i):
+        spot = g_all.at[i, :, lane_band(x)]
+        return remote(spot, spot, 3, i, 0, z * n_x + x_peer)
+
+    def give(i, value):
+        if fuse:
+            g_send[i] = value.astype(BF16)
+            to_x(i).start()
+        else:
+            grads_out[i] = value
+
+    def phase_z(i):
+        to_x(i).wait()
+        g_part[i] = (
+            g_send[i, :, lane_band(x)].astype(F32) + g_x[i].astype(F32)
+        ).astype(BF16)
+        for d in range(1, n_z):
+            to_z(i, d).start()
+
+    def phase_sum(i):
+        for d in range(1, n_z):
+            to_z(i, d).wait()
+        value = g_part[i, row_band(z)].astype(F32)
+        for d in range(1, n_z):
+            value = value + g_z[i, d].astype(F32)
+        g_all[i, row_band(z), lane_band(x)] = value.astype(BF16)
+        for d in range(1, n_z):
+            out_z(i, d).start()
+
+    def phase_x(i):
+        for d in range(1, n_z):
+            out_z(i, d).wait()
+        out_x(i).start()
+
+    def phase_end(i):
+        out_x(i).wait()
+        grads_out[i] = g_all[i].astype(F32)
+
+    give(3, nt(att_own[...], d_attn))
     d_att = nn(wo_in[...], d_attn).astype(BF16)
 
     flip = (
@@ -371,35 +508,81 @@
         padded = jnp.concatenate([flipped, jnp.zeros_like(flipped)], axis=1)
         turned = pltpu.roll(padded, 0, 1, stride=1, stride_axis=0)
         line = jnp.sum(turned, axis=0, keepdims=True)
-        gtable_out[:, h : h + 1] = jnp.sum(onehot * line, axis=1, keepdims=True)
-
-    d_n1 = nn(wq[...], dq_s[...]) + nn(wk[...], dk_s[...]) + nn(wv[...], dv_s[...])
+        line8 = jnp.broadcast_to(line, (8, 2 * length))
+        high = line8.astype(BF16)
+        rest = (line8 - high.astype(F32)).astype(BF16)
+        sums = nt(high, onehot.astype(BF16)) + nt(rest, onehot.astype(BF16))
+        tiny_s[n_exp + 16 + h : n_exp + 17 + h, :buckets] = sums[:1]
+
+    give(2, nt(dv_s[...], n1_s[...]))
+    if fuse:
+        phase_z(3)
+    give(1, nt(dk_s[...], n1_s[...]))
+    give(0, nt(dq_s[...], n1_s[...]))
+    d_n1 = tn(wq[...], dq_s[...]) + tn(wk[...], dk_s[...]) + tn(wv[...], dv_s[...])
     xf = x_all[...].astype(F32)
     stat = jnp.sum(d_n1 * gain1 * xf * inv_one, axis=0, keepdims=True)
     for p in range(n_mp):
-        dn_send[p, :cs] = d_n1[p * cs : (p + 1) * cs].astype(BF16)
-        dn_send[p, cs:] = jnp.broadcast_to(stat, (16, length)).astype(BF16)
-    lasts = []
-    for d in range(1, n_mp):
-        copy = to_mp(
-            dn_send.at[lax.rem(m + d, n_mp)], dn_recv.at[d], s8.at[d], r8.at[d], d
-        )
-        copy.start()
-        lasts.append(copy)
-    gq_out[...] = nt(n1_s[...], dq_s[...])
-    gk_out[...] = nt(n1_s[...], dk_s[...])
-    gv_out[...] = nt(n1_s[...], dv_s[...])
-    for copy in lasts:
-        copy.wait()
-    both = dn_send[m].astype(F32)
-    for d in range(1, n_mp):
-        both = both + dn_recv[d].astype(F32)
+        q = (p % 2) * 2 + p // 2
+        dn_send[q, :cs] = d_n1[p * cs : (p + 1) * cs].astype(BF16)
+        dn_send[q, cs:] = jnp.broadcast_to(stat, (16, length)).astype(BF16)
+    first, second = halve(dn_send, dn_recv, dn_b, dn_c, s8, r8)
+    first.start()
+    if fuse:
+        phase_z(2)
+    first.wait()
+    dn_b[...] = (dn_send[across_quarter].astype(F32) + dn_recv[1 - side].astype(F32)).astype(BF16)
+    second.start()
+    both = dn_send[quarter].astype(F32) + dn_recv[side].astype(F32)
+    if fuse:
+        phase_z(1)
+        phase_sum(3)
+        phase_z(0)
+    second.wait()
+    both = both + dn_c[...].astype(F32)
     d_own = both[:cs]
     mean_own = both[cs : cs + 1] / width
     hat_one = x_in[...].astype(F32) * inv_one
-    gain1_own = small_in[:, n_exp : n_exp + 1].astype(F32)
+    gain1_own = turn_s[own, n_exp : n_exp + 1]
     gtok_out[...] = dres_s[own] + inv_one * (d_own * gain1_own - hat_one * mean_own)
-    ggain1_out[...] = jnp.sum(d_own * hat_one, axis=1, keepdims=True)
+    tiny_s[n_exp + 8 : n_exp + 16, :cs] = lane_sums(d_own * hat_one)
+    if not fuse:
+        tiny_out[...] = tiny_s[...]
+        return
+
+    def tiny_copy(src, dst, d, where):
+        return pltpu.make_async_remote_copy(
+            src_ref=src,
+            dst_ref=dst,
+            send_sem=s10.at[d],
+            recv_sem=r10.at[d],
+            device_id=(where, m),
+            device_id_type=MESH,
+        )
+
+    def tiny_over(d):
+        return tiny_copy(tiny_b, tiny_z.at[d], d, lax.rem(z + d, n_z) * n_x + x)
+
+    pair = tiny_copy(tiny_s, tiny_x, 0, z * n_x + x_peer)
+    pair.start()
+    phase_sum(2)
+    phase_sum(1)
+    phase_x(3)
+    pair.wait()
+    tiny_b[...] = tiny_s[...] + tiny_x[...]
+    for d in range(1, n_z):
+        tiny_over(d).start()
+    phase_sum(0)
+    for i in (2, 1, 0):
+        phase_x(i)
+    for d in range(1, n_z):
+        tiny_over(d).wait()
+    value = tiny_b[...]
+    for d in range(1, n_z):
+        value = value + tiny_z[d]
+    tiny_out[...] = value
+    for i in (3, 2, 1, 0):
+        phase_end(i)
 
 
 def body(
@@ -430,7 +613,18 @@
     hid = w_in.shape[2]
     heads = cs // HEAD_DIM
     buckets = bias_table.shape[0]
-    small = jnp.concatenate([w_router, gain_one[:, None], gain_two[:, None]], axis=1)
+    n_small = -(-(n_exp + 2) // 16) * 16
+    small = jnp.concatenate(
+        [
+            w_router.T,
+            gain_one[None],
+            gain_two[None],
+            jnp.zeros((n_small - n_exp - 2, cs), BF16),
+        ]
+    )
+    n_x = 2
+    n_z = max(1, n_exp // n_x) if n_exp == 8 else 1
+    n_tiny = n_exp + 24
     bucket_rev = jnp.concatenate(
         [bucket[::-1], jnp.full((1,), -1, jnp.int32)]
     )[None, :]
@@ -438,28 +632,22 @@
     vm = pltpu.VMEM
     dma = pltpu.SemaphoreType.DMA
     outs = pl.pallas_call(
-        functools.partial(kernel, n_exp, cap),
+        functools.partial(kernel, n_exp, cap, n_x),
         out_shape=(
             sds((cs, length), BF16),
             sds((cs, length), F32),
-            sds((cs, 1), F32),
-            sds((cs, 1), F32),
-            sds((width, cs), F32),
-            sds((width, cs), F32),
-            sds((width, cs), F32),
-            sds((cs, width), F32),
-            sds((buckets, heads), F32),
-            sds((cs, n_exp), F32),
+            sds((4, cs, width), F32),
+            sds((n_tiny, width), F32),
             sds((4, n_exp, cap, half), BF16),
             sds((rows, hid), BF16),
             sds((rows, hid), BF16),
         ),
         in_specs=[pl.BlockSpec(memory_space=vm)] * 13,
-        out_specs=tuple([pl.BlockSpec(memory_space=vm)] * 13),
+        out_specs=tuple([pl.BlockSpec(memory_space=vm)] * 7),
         scratch_shapes=[
             vm((width, length), BF16),
             vm((width, length), BF16),
-            vm((width, n_exp + 2), BF16),
+            vm((4, n_small, cs), BF16),
             vm((width, width), BF16),
             vm((cs, length), BF16),
             vm((width, length), BF16),
@@ -472,19 +660,31 @@
             vm((4, half, length), BF16),
             vm((n_exp, cap, half), BF16),
             vm((4, rows, half), BF16),
-            vm((4, rows, half), BF16),
+            vm((2, rows, half), BF16),
             vm((n_exp, cap, half), BF16),
             vm((n_exp, cap, half), BF16),
             vm((half, length), BF16),
             vm((4 * half, length), BF16),
-            vm((width, 1), F32),
-            vm((width, n_exp), F32),
             vm((width, length), F32),
+            vm((width, n_small), F32),
             vm((cs, length), BF16),
             vm((cs, length), BF16),
             vm((cs, length), BF16),
+            vm((rows, half), BF16),
+            vm((rows, half), BF16),
             vm((4, cs + 16, length), BF16),
-            vm((4, cs + 16, length), BF16),
+            vm((2, cs + 16, length), BF16),
+            vm((cs + 16, length), BF16),
+            vm((cs + 16, length), BF16),
+            vm((4, cs, width), BF16),
+            vm((4, cs, half), BF16),
+            vm((4, cs, half), BF16),
+            vm((4, n_z, cs // n_z, half), BF16),
+            vm((4, cs, width), BF16),
+            vm((n_tiny, width), F32),
+            vm((n_tiny, width), F32),
+            vm((n_tiny, width), F32),
+            vm((n_z, n_tiny, width), F32),
             dma((4, 4)),
             dma((4, 4)),
             dma((4,)),
@@ -501,6 +701,10 @@
             dma((4,)),
             dma((4,)),
             dma((4,)),
+            dma((4, 4, n_z)),
+            dma((4, 4, n_z)),
+            dma((n_z,)),
+            dma((n_z,)),
         ],
         compiler_params=pltpu.CompilerParams(
             collective_id=0, has_side_effects=True, vmem_limit_bytes=60 * 2**20
@@ -509,9 +713,9 @@
         tokens.T,
         cotangent.T,
         small,
-        w_query,
-        w_key,
-        w_value,
+        w_query.T,
+        w_key.T,
+        w_value.T,
         w_out,
         bias_table,
         w_in[0],
@@ -520,25 +724,28 @@
         slot_index[None, :],
         bucket_rev,
     )
-    mixed, gtok, gg1, gg2, gq, gk, gv, gout, gtable, grouter, blocks, hidden, d_pre = outs
+    mixed, gtok, grads, tiny, blocks, hidden, d_pre = outs
     flat = blocks.reshape(4, rows, half)
     grad_in = jnp.einsum("hsd,sf->hdf", flat[:2], d_pre, preferred_element_type=F32).reshape(
         width, hid
     )
     d_rows = jnp.concatenate([flat[2], flat[3]], axis=1)
     grad_eo = jnp.einsum("sf,sd->fd", hidden, d_rows, preferred_element_type=F32)
-    summed = lax.psum((gq, gk, gv, gout, gtable, grouter, gg1[:, 0], gg2[:, 0]), "expert")
+    if n_exp != 8:
+        grads, tiny = lax.psum((grads, tiny), "expert")
+    first = lax.axis_index("mp") * cs
+    shared = lax.dynamic_slice_in_dim(tiny[: n_exp + 1], first, cs, 1)
     return (
         mixed.T,
         gtok.T,
-        summed[6],
-        summed[7],
-        summed[0],
-        summed[1],
-        summed[2],
-        summed[3],
-        summed[4],
-        summed[5],
+        tiny[n_exp + 8, :cs],
+        shared[n_exp],
+        grads[0].T,
+        grads[1].T,
+        grads[2].T,
+        grads[3],
+        tiny[n_exp + 16 : n_exp + 16 + heads, :buckets].T,
+        shared[:n_exp].T,
         grad_in[None],
         grad_eo[None],
     )

time: 258 us -> 140 us (0.54)
  waiting for transfers between devices: 78.8 us -> 0 us
  blocking collectives: 43.4 us -> 0 us
  Pallas kernels: 97.8 us -> 117 us
  between operations: 14.2 us -> 0.68 us
  local copies, waits for them, and re-layouts: 17.5 us -> 14.8 us
    psum x1 -> x0, waiting for transfers between devices: 78.7 us -> none  [body(): lax.psum((gq, gk, gv, gout, gtable, grouter, gg1[:, 0], gg2[:, 0]), 'expe...]
    psum x1 -> x0, blocking collectives: 43.4 us -> none  [body(): lax.psum((gq, gk, gv, gout, gtable, grouter, gg1[:, 0], gg2[:, 0]), 'expe...]
    pallas_call x1, Pallas kernels: 97.8 us -> 117 us  [body(): pl.pallas_call(functools.partial(kernel, n_exp, cap, n_x), out_shape=(sds...]
    unnamed x44 -> x15, local copies, waits for them, and re-layouts: 15 us -> 5.22 us
    squeeze x0 -> x1, local copies, waits for them, and re-layouts: none -> 3.13 us  [body(): grads[3]]
    slice x0 -> x3, local copies, waits for them, and re-layouts: none -> 2.7 us  [the longest x1 1.26 us: body(): tiny[n_exp + 8, :cs]]
  transfers between devices with their start and end apart: 1 -> 0, of which waited for: 1 -> 0; matrix products, arithmetic and copies ran while one was open for 2% -> 0% of each run, Pallas kernels for 0% -> 0%
where the time goes in v2:
time: 140 us; the launch traced here: 139 us
  Pallas kernels  117 us (84%)
  local copies, waits for them, and re-layouts  14.8 us (11%)
  matrix products  4.38 us (3%)
  other arithmetic  2.01 us (1%)
    pallas_call x1, Pallas kernels, body(): pl.pallas_call(functools.partial(kernel, n_exp, cap, n_x), out_shape=(sds...  117 us
    unnamed x15, local copies, waits for them, and re-layouts  5.22 us
    squeeze x1, local copies, waits for them, and re-layouts, body(): grads[3]  3.13 us

profile of v2, /device:TPU:0, one launch (start us, length us, event | category | flops | bytes accessed | tf_op | source)
XLA Modules:
  0.0 139.4 jit_solution(10328924342552921057)
XLA Ops:
  0.6 0.7 broadcast_in_dim.22
  1.3 0.7 broadcast_in_dim.21
  2.0 0.1 pad.7.clone
  2.0 1.4 maximum_maximum_fusion.small_in
  3.4 1.4 copy.28.table
  4.8 0.8 reverse
  5.5 0.1 slice.59
  5.6 0.7 pad_add_fusion
  6.3 117.5 %shard_map.238 = (bf16[192,256]{1,0:T(8,128)(2,1)}, f32[192,256]{1,0:T(8,128)}, f32[4,192,768]{2,1,0:T(8,128)}, f32[32,768]{1,0:T(8,128)}, bf16[4,8,48,384]{3,2,...) custom-call(bf16[192,256]{1,0:T(8,128)(2,1)} %bitcast.58, bf16[192,256]{1,0:T(8,128)(2,1)} %bitcast.59, ...), custom_call_target="tpu_custom_call" | custom-call | tf_op jit(solution)/shard_map/pallas_call | solution.py:634
  123.8 1.3 slice.41
  125.0 0.8 slice.42
  125.8 0.6 dynamic-slice
  126.5 0.0 copy-start
  126.5 3.1 %slice_bitcast_fusion = (f32[192,768]{1,0:T(8,128)}, f32[768,192]{0,1:T(8,128)}, f32[768,192]{0,1:T(8,128)}, f32[768,192]{0,1:T(8,128)}) fusion(f32[4,192,768]{2,1,0:T(8,128)} %get-tuple-element.22), kind=kLoop, calls=%fused_computation.5 | loop fusion | bytes 4718592 | tf_op jit(solution)/shard_map/squeeze | solution.py:746
  129.6 1.2 slice_bitcast_fusion.4
  130.8 0.7 dynamic-slice_bitcast_fusion
  131.5 0.0 copy-done
  131.5 0.0 copy-start.2
  131.5 0.1 slice.50
  131.6 0.3 copy.29
  131.9 0.7 copy-done.2
  132.6 2.2 %convolution_bitcast_fusion.1 = f32[1,768,768]{2,1,0:T(8,128)} fusion(bf16[768,384]{1,0:T(8,128)(2,1)S(1)} %bitcast.47, bf16[384,768]{1,0:T(8,128)(2,1)S(1)} %copy-done.2), kind=kOutput, calls=%fused_computation.1 | convolution fusion | flops 452984832 | bytes 3538944 | tf_op jit(solution)/shard_map/hsd,sf->hdf/dot_general | solution.py:729
  134.8 0.0 copy-start.1
  134.8 0.1 fusion.4
  134.8 1.0 copy-done.1
  135.8 0.0 copy-start.4
  135.8 0.0 copy-start.3
  135.8 2.2 %convolution_bitcast_fusion = f32[1,768,768]{2,1,0:T(8,128)} fusion(bf16[384,768]{1,0:T(8,128)(2,1)S(1)} %copy-done.1, bf16[384,384]{1,0:T(8,128)(2,1)S(1)} %bitcast.50, bf16[384,384]{1,0:T(8,128)(2,1)S(1)} %bitcast.49), kind=kOutput, calls=%fused_computation | convolution fusion | flops 454164480 | bytes 3538944 | tf_op jit(solution)/shard_map/sf,sd->fd/dot_general | solution.py:733
  138.0 0.0 copy-done.4
  138.0 0.6 copy.32
  138.7 0.0 copy-done.3
  138.7 0.7 copy.33
  (1 shorter events, 0.0 us)
Async XLA Ops:
  126.5 5.1 %copy-start = (bf16[4,8,48,384]{3,2,1,0:T(8,128)(2,1)S(1)}, bf16[4,8,48,384]{3,2,1,0:T(8,128)(2,1)}, u32[]{:S(2)}) copy-start(bf16[4,8,48,384]{3,2,1,0:T(8,128)(2,1)} %get-tuple-element.23) | copy-start | bytes 3538948
  131.5 1.1 copy-start.2
  134.8 1.1 copy-start.1
  135.8 2.2 %copy-start.4 = (bf16[192,256]{1,0:T(8,128)(2,1)S(1)}, bf16[192,256]{1,0:T(8,128)(2,1)}, u32[]{:S(2)}) copy-start(bf16[192,256]{1,0:T(8,128)(2,1)} %get-tuple-element.19) | copy-start | bytes 294916
  135.8 2.9 %copy-start.3 = (f32[192,256]{1,0:T(8,128)S(1)}, f32[192,256]{1,0:T(8,128)}, u32[]{:S(2)}) copy-start(f32[192,256]{1,0:T(8,128)} %get-tuple-element.20) | copy-start | bytes 589828

commit v3 on v2

--- a/solution.py
+++ b/solution.py
@@ -32,7 +32,9 @@
     n_x,
     x_in,
     cot_in,
-    small_in,
+    router_in,
+    gain1_in,
+    gain2_in,
     wq,
     wk,
     wv,
@@ -45,7 +47,10 @@
     bucket_rev,
     mixed_out,
     gtok_out,
-    grads_out,
+    gq_out,
+    gk_out,
+    gv_out,
+    gout_out,
     tiny_out,
     rows_out,
     hidden_out,
@@ -72,6 +77,9 @@
     ret_all,
     dres_s,
     turn_s,
+    small_f,
+    small_in,
+    tiny_h,
     dq_s,
     dk_s,
     dv_s,
@@ -191,6 +199,12 @@
         return pl.ds(pl.multiple_of(p * cs, cs), cs)
 
     own = band(m)
+    grads_out = (gq_out, gk_out, gv_out, gout_out)
+    small_f[...] = jnp.zeros_like(small_f)
+    small_f[:n_exp] = router_in[...].astype(F32)
+    small_f[n_exp : n_exp + 1] = gain1_in[...].astype(F32)
+    small_f[n_exp + 1 : n_exp + 2] = gain2_in[...].astype(F32)
+    small_in[...] = small_f[...].astype(BF16)
     small_all[m] = small_in[...]
     trios = [
         spread(x_in, x_all, band, s1.at[0], r1.at[0]),
@@ -198,20 +212,20 @@
         spread(wo_in, wo_all, band, s1.at[2], r1.at[2]),
         spread(cot_in, cot_all, band, s1.at[3], r1.at[3]),
     ]
-    for trio in trios:
+    for trio in trios[:2]:
         begin(trio)
     x_all[own] = x_in[...]
     wo_all[own] = wo_in[...]
     cot_all[own] = cot_in[...]
 
-    buckets = table.shape[0]
+    buckets = table.shape[1]
     onehot = (
         lax.broadcasted_iota(jnp.int32, (buckets, 2 * length), 0) == bucket_rev[...]
     ).astype(F32)
-    table_f = table[...].astype(F32)
+    lines = nn(table[...], onehot.astype(BF16))
 
     def head_bias(h):
-        line = jnp.sum(table_f[:, h : h + 1] * onehot, axis=0, keepdims=True)
+        line = lines[h : h + 1]
         spread = jnp.broadcast_to(line, (length, 2 * length))
         turned = pltpu.roll(spread, length + 1, 1, stride=1, stride_axis=0)
         return turned[:, :length]
@@ -221,6 +235,8 @@
 
     for trio in trios[:2]:
         pass_on(trio)
+    for trio in trios[2:]:
+        begin(trio)
     for trio in trios[:2]:
         finish(trio)
     n_small = small_in.shape[0]
@@ -407,7 +423,7 @@
     n2_again = (hat_two * gain2).astype(BF16)
     tiny_s[:n_exp] = nt(d_logits, n2_again)
     d_n2 = ret_all[width:].astype(F32) + nn(router, d_logits)
-    tiny_s[n_exp : n_exp + 8] = lane_sums(d_n2 * hat_two)
+    tiny_s[n_exp : n_exp + 1] = lane_sums(d_n2 * hat_two)[:1]
     u_two = d_n2 * gain2
     d_resid = cot_f + inv_two * (
         u_two - hat_two * (jnp.sum(u_two * hat_two, axis=0, keepdims=True) / width)
@@ -457,7 +473,7 @@
             g_send[i] = value.astype(BF16)
             to_x(i).start()
         else:
-            grads_out[i] = value
+            grads_out[i][...] = value
 
     def phase_z(i):
         to_x(i).wait()
@@ -484,7 +500,7 @@
 
     def phase_end(i):
         out_x(i).wait()
-        grads_out[i] = g_all[i].astype(F32)
+        grads_out[i][...] = g_all[i].astype(F32)
 
     give(3, nt(att_own[...], d_attn))
     d_att = nn(wo_in[...], d_attn).astype(BF16)
@@ -512,13 +528,17 @@
         high = line8.astype(BF16)
         rest = (line8 - high.astype(F32)).astype(BF16)
         sums = nt(high, onehot.astype(BF16)) + nt(rest, onehot.astype(BF16))
-        tiny_s[n_exp + 16 + h : n_exp + 17 + h, :buckets] = sums[:1]
+        tiny_s[n_exp + 2 + h : n_exp + 3 + h, :buckets] = sums[:1]
+        if fuse and h == heads - 2:
+            phase_z(3)
 
     give(2, nt(dv_s[...], n1_s[...]))
+    give(1, nt(dk_s[...], n1_s[...]))
     if fuse:
-        phase_z(3)
-    give(1, nt(dk_s[...], n1_s[...]))
+        phase_sum(3)
     give(0, nt(dq_s[...], n1_s[...]))
+    if fuse:
+        phase_z(2)
     d_n1 = tn(wq[...], dq_s[...]) + tn(wk[...], dk_s[...]) + tn(wv[...], dv_s[...])
     xf = x_all[...].astype(F32)
     stat = jnp.sum(d_n1 * gain1 * xf * inv_one, axis=0, keepdims=True)
@@ -529,14 +549,13 @@
     first, second = halve(dn_send, dn_recv, dn_b, dn_c, s8, r8)
     first.start()
     if fuse:
-        phase_z(2)
+        phase_z(1)
     first.wait()
     dn_b[...] = (dn_send[across_quarter].astype(F32) + dn_recv[1 - side].astype(F32)).astype(BF16)
     second.start()
     both = dn_send[quarter].astype(F32) + dn_recv[side].astype(F32)
     if fuse:
-        phase_z(1)
-        phase_sum(3)
+        phase_x(3)
         phase_z(0)
     second.wait()
     both = both + dn_c[...].astype(F32)
@@ -545,7 +564,7 @@
     hat_one = x_in[...].astype(F32) * inv_one
     gain1_own = turn_s[own, n_exp : n_exp + 1]
     gtok_out[...] = dres_s[own] + inv_one * (d_own * gain1_own - hat_one * mean_own)
-    tiny_s[n_exp + 8 : n_exp + 16, :cs] = lane_sums(d_own * hat_one)
+    tiny_s[n_exp + 1 : n_exp + 2, :cs] = lane_sums(d_own * hat_one)[:1]
     if not fuse:
         tiny_out[...] = tiny_s[...]
         return
@@ -563,25 +582,28 @@
     def tiny_over(d):
         return tiny_copy(tiny_b, tiny_z.at[d], d, lax.rem(z + d, n_z) * n_x + x)
 
-    pair = tiny_copy(tiny_s, tiny_x, 0, z * n_x + x_peer)
+    tiny_h[...] = tiny_s[...].astype(BF16)
+    pair = tiny_copy(tiny_h, tiny_x, 0, z * n_x + x_peer)
     pair.start()
     phase_sum(2)
     phase_sum(1)
-    phase_x(3)
     pair.wait()
-    tiny_b[...] = tiny_s[...] + tiny_x[...]
+    tiny_b[...] = (tiny_s[...] + tiny_x[...].astype(F32)).astype(BF16)
     for d in range(1, n_z):
         tiny_over(d).start()
+    phase_x(2)
     phase_sum(0)
-    for i in (2, 1, 0):
-        phase_x(i)
+    phase_x(1)
+    phase_end(3)
+    phase_end(2)
+    phase_x(0)
     for d in range(1, n_z):
         tiny_over(d).wait()
-    value = tiny_b[...]
+    value = tiny_b[...].astype(F32)
     for d in range(1, n_z):
-        value = value + tiny_z[d]
+        value = value + tiny_z[d].astype(F32)
     tiny_out[...] = value
-    for i in (3, 2, 1, 0):
+    for i in (1, 0):
         phase_end(i)
 
 
@@ -614,17 +636,9 @@
     heads = cs // HEAD_DIM
     buckets = bias_table.shape[0]
     n_small = -(-(n_exp + 2) // 16) * 16
-    small = jnp.concatenate(
-        [
-            w_router.T,
-            gain_one[None],
-            gain_two[None],
-            jnp.zeros((n_small - n_exp - 2, cs), BF16),
-        ]
-    )
     n_x = 2
     n_z = max(1, n_exp // n_x) if n_exp == 8 else 1
-    n_tiny = n_exp + 24
+    n_tiny = -(-(n_exp + 2 + heads) // 16) * 16
     bucket_rev = jnp.concatenate(
         [bucket[::-1], jnp.full((1,), -1, jnp.int32)]
     )[None, :]
@@ -636,14 +650,17 @@
         out_shape=(
             sds((cs, length), BF16),
             sds((cs, length), F32),
-            sds((4, cs, width), F32),
+            sds((cs, width), F32),
+            sds((cs, width), F32),
+            sds((cs, width), F32),
+            sds((cs, width), F32),
             sds((n_tiny, width), F32),
             sds((4, n_exp, cap, half), BF16),
             sds((rows, hid), BF16),
             sds((rows, hid), BF16),
         ),
-        in_specs=[pl.BlockSpec(memory_space=vm)] * 13,
-        out_specs=tuple([pl.BlockSpec(memory_space=vm)] * 7),
+        in_specs=[pl.BlockSpec(memory_space=vm)] * 15,
+        out_specs=tuple([pl.BlockSpec(memory_space=vm)] * 10),
         scratch_shapes=[
             vm((width, length), BF16),
             vm((width, length), BF16),
@@ -667,6 +684,9 @@
             vm((4 * half, length), BF16),
             vm((width, length), F32),
             vm((width, n_small), F32),
+            vm((n_small, cs), F32),
+            vm((n_small, cs), BF16),
+            vm((n_tiny, width), BF16),
             vm((cs, length), BF16),
             vm((cs, length), BF16),
             vm((cs, length), BF16),
@@ -682,9 +702,9 @@
             vm((4, n_z, cs // n_z, half), BF16),
             vm((4, cs, width), BF16),
             vm((n_tiny, width), F32),
-            vm((n_tiny, width), F32),
-            vm((n_tiny, width), F32),
-            vm((n_z, n_tiny, width), F32),
+            vm((n_tiny, width), BF16),
+            vm((n_tiny, width), BF16),
+            vm((n_z, n_tiny, width), BF16),
             dma((4, 4)),
             dma((4, 4)),
             dma((4,)),
@@ -712,19 +732,21 @@
     )(
         tokens.T,
         cotangent.T,
-        small,
+        w_router.T,
+        gain_one[None],
+        gain_two[None],
         w_query.T,
         w_key.T,
         w_value.T,
         w_out,
-        bias_table,
+        bias_table.T,
         w_in[0],
         w_exp_out[0],
         routes[None, :],
         slot_index[None, :],
         bucket_rev,
     )
-    mixed, gtok, grads, tiny, blocks, hidden, d_pre = outs
+    mixed, gtok, *grads, tiny, blocks, hidden, d_pre = outs
     flat = blocks.reshape(4, rows, half)
     grad_in = jnp.einsum("hsd,sf->hdf", flat[:2], d_pre, preferred_element_type=F32).reshape(
         width, hid
@@ -738,13 +760,13 @@
     return (
         mixed.T,
         gtok.T,
-        tiny[n_exp + 8, :cs],
+        tiny[n_exp + 1, :cs],
         shared[n_exp],
         grads[0].T,
         grads[1].T,
         grads[2].T,
         grads[3],
-        tiny[n_exp + 16 : n_exp + 16 + heads, :buckets].T,
+        tiny[n_exp + 2 : n_exp + 2 + heads, :buckets].T,
         shared[:n_exp].T,
         grad_in[None],
         grad_eo[None],

time: 140 us -> 135 us (0.964)
  Pallas kernels: 117 us -> 113 us
    pallas_call x1, Pallas kernels: 117 us -> 113 us  [body(): pl.pallas_call(functools.partial(kernel, n_exp, cap, n_x), out_shape=(sds...]
    squeeze x1 -> x0, local copies, waits for them, and re-layouts: 3.13 us -> none  [body(): grads[3]]
    unnamed x15 -> x26, local copies, waits for them, and re-layouts: 5.22 us -> 6.12 us
where the time goes in v3:
time: 135 us; the launch traced here: 134 us
  Pallas kernels  113 us (84%)
  local copies, waits for them, and re-layouts  15.4 us (11%)
  matrix products  4.38 us (3%)
    pallas_call x1, Pallas kernels, body(): pl.pallas_call(functools.partial(kernel, n_exp, cap, n_x), out_shape=(sds...  113 us
    unnamed x26, local copies, waits for them, and re-layouts  6.12 us

profile of v3, /device:TPU:0, one launch (start us, length us, event | category | flops | bytes accessed | tf_op | source)
XLA Modules:
  0.0 134.1 jit_solution(10056110397557592714)
XLA Ops:
  0.6 1.2 broadcast_in_dim.18.gain1_in
  1.9 1.2 broadcast_in_dim.19.gain2_in
  3.1 0.8 reverse
  3.9 0.1 slice.39
  3.9 0.7 pad_add_fusion
  4.6 113.0 %shard_map.238 = (bf16[192,256]{1,0:T(8,128)(2,1)}, f32[192,256]{1,0:T(8,128)}, f32[192,768]{1,0:T(8,128)}, f32[192,768]{1,0:T(8,128)}, f32[192,768]{1,0:T(8,128...) custom-call(bf16[192,256]{1,0:T(8,128)(2,1)} %bitcast.52, ...), custom_call_target="tpu_custom_call" | custom-call | tf_op jit(solution)/shard_map/pallas_call | solution.py:648
  117.6 0.0 copy-start
  117.6 1.4 %dynamic-slice = f32[1,192]{1,0:T(1,128)} dynamic-slice(f32[9,768]{1,0:T(8,128)} %bitcast.56, s32[]{:T(128)S(6)} %add.5, s32[]{:T(128)S(6)} %select_n.3), dynamic_slice_sizes={1,192} | dynamic-slice | bytes 1540 | tf_op jit(solution)/shard_map/slice | solution.py:764
  119.0 1.3 slice.29
  120.3 1.3 slice_bitcast_fusion
  121.5 1.4 %dynamic-slice_bitcast_fusion = f32[192,8]{0,1:T(8,128)} fusion(f32[9,768]{1,0:T(8,128)} %bitcast.57, s32[]{:T(128)S(6)} %select_n.3), kind=kLoop, calls=%fused_computation.5 | loop fusion | bytes 12292 | tf_op jit(solution)/shard_map/transpose | solution.py:770
  122.9 1.1 slice.34
  124.0 0.0 copy-done
  124.0 0.0 copy-start.2
  124.1 0.1 fusion.4
  124.1 0.3 copy.27
  124.4 0.7 copy-done.2
  125.1 0.0 copy-start.1
  125.1 2.2 %convolution_bitcast_fusion.1 = f32[1,768,768]{2,1,0:T(8,128)} fusion(bf16[768,384]{1,0:T(8,128)(2,1)S(1)} %bitcast.38, bf16[384,768]{1,0:T(8,128)(2,1)S(1)} %copy-done.2), kind=kOutput, calls=%fused_computation.1 | convolution fusion | flops 452984832 | bytes 3538944 | tf_op jit(solution)/shard_map/hsd,sf->hdf/dot_general | solution.py:751
  127.3 0.0 copy-done.1
  127.3 0.0 copy-start.8
  127.3 0.0 copy-start.7
  127.3 0.0 copy-start.6
  127.3 2.2 %convolution_bitcast_fusion = f32[1,768,768]{2,1,0:T(8,128)} fusion(bf16[384,768]{1,0:T(8,128)(2,1)S(1)} %copy-done.1, bf16[384,384]{1,0:T(8,128)(2,1)S(1)} %bitcast.41, bf16[384,384]{1,0:T(8,128)(2,1)S(1)} %bitcast.40), kind=kOutput, calls=%fused_computation | convolution fusion | flops 454164480 | bytes 3538944 | tf_op jit(solution)/shard_map/sf,sd->fd/dot_general | solution.py:755
  129.5 0.0 copy-done.8
  129.5 0.0 copy-start.5
  129.5 0.6 copy.34
  130.2 0.0 copy-done.7
  130.2 0.7 copy.35
  130.8 0.0 copy-done.6
  130.8 0.0 copy-start.4
  130.8 0.8 copy.36
  131.7 0.0 copy-done.5
  131.7 0.0 copy-start.3
  131.7 0.8 copy.37
  132.5 0.0 copy-done.4
  132.5 0.8 copy.38
  133.3 0.0 copy-done.3
  133.3 0.8 copy.39
Async XLA Ops:
  117.6 6.5 %copy-start = (bf16[4,8,48,384]{3,2,1,0:T(8,128)(2,1)S(1)}, bf16[4,8,48,384]{3,2,1,0:T(8,128)(2,1)}, u32[]{:S(2)}) copy-start(bf16[4,8,48,384]{3,2,1,0:T(8,128)(2,1)} %get-tuple-element.29) | copy-start | bytes 3538948
  124.0 1.1 copy-start.2
  125.1 2.2 %copy-start.1 = (bf16[384,768]{1,0:T(8,128)(2,1)S(1)}, bf16[384,768]{1,0:T(8,128)(2,1)}, u32[]{:S(2)}) copy-start(bf16[384,768]{1,0:T(8,128)(2,1)} %get-tuple-element.31) | copy-start | bytes 1769476
  127.3 2.2 %copy-start.8 = (bf16[192,256]{1,0:T(8,128)(2,1)S(1)}, bf16[192,256]{1,0:T(8,128)(2,1)}, u32[]{:S(2)}) copy-start(bf16[192,256]{1,0:T(8,128)(2,1)} %get-tuple-element.22) | copy-start | bytes 294916
  127.3 2.9 %copy-start.7 = (f32[192,256]{1,0:T(8,128)S(1)}, f32[192,256]{1,0:T(8,128)}, u32[]{:S(2)}) copy-start(f32[192,256]{1,0:T(8,128)} %get-tuple-element.23) | copy-start | bytes 589828
  127.3 3.5 %copy-start.6 = (f32[192,768]{1,0:T(8,128)S(1)}, f32[192,768]{1,0:T(8,128)}, u32[]{:S(2)}) copy-start(f32[192,768]{1,0:T(8,128)} %get-tuple-element.25) | copy-start | bytes 1769476
  129.5 2.1 %copy-start.5 = (f32[192,768]{1,0:T(8,128)S(1)}, f32[192,768]{1,0:T(8,128)}, u32[]{:S(2)}) copy-start(f32[192,768]{1,0:T(8,128)} %get-tuple-element.26) | copy-start | bytes 1769476
  130.8 1.6 %copy-start.4 = (f32[192,768]{1,0:T(8,128)S(1)}, f32[192,768]{1,0:T(8,128)}, u32[]{:S(2)}) copy-start(f32[192,768]{1,0:T(8,128)} %get-tuple-element.27) | copy-start | bytes 1769476
  131.7 1.6 %copy-start.3 = (f32[192,768]{1,0:T(8,128)S(1)}, f32[192,768]{1,0:T(8,128)}, u32[]{:S(2)}) copy-start(f32[192,768]{1,0:T(8,128)} %get-tuple-element.53) | copy-start | bytes 1769476
